TPU v7x, 128 devices: a whole 4x4x4 slice. The times are simulated.
128 devices in a mesh: dp: 8 (over x, core), expert: 16 (over z, y).
Axes of the slice: x: 4, y: 4, z: 4, core: 2. Of those that a mesh axis runs over, the one named last changes fastest.
Arguments:
- x_saved: bfloat16 [8, 32, 1280, 1024], P('dp', 'expert'), may hold values from -6 to 6
- d_out: bfloat16 [32768, 1024], P(('dp', 'expert')), may hold values from -6 to 6
- routes: int32 [32768, 8], P(('dp', 'expert')), may hold values from 0 to 31, all different within a row; in each aligned block of 256 rows (0 to 255, 256 to 511, ...) at most 80 rows name the same one
- probs: float32 [32768, 8], P(('dp', 'expert')), may hold values from 0.1 to 0.9
- w_gate: bfloat16 [32, 1024, 512], P('expert'), may hold values from -0.1875 to 0.1875
- w_up: bfloat16 [32, 1024, 512], P('expert'), may hold values from -0.1875 to 0.1875
- w_down: bfloat16 [32, 512, 1024], P('expert'), may hold values from -0.25 to 0.25
- res_gate: bfloat16 [8, 32, 1024, 512], P('dp', 'expert'), may hold values from -6 to 6
- res_up: bfloat16 [8, 32, 1024, 512], P('dp', 'expert'), may hold values from -6 to 6
- res_down: bfloat16 [8, 32, 512, 1024], P('dp', 'expert'), may hold values from -1.5 to 1.5
Outputs:
- d_tokens: bfloat16 [32768, 1024], P(('dp', 'expert'))
- grad_gate: float32 [32, 1024, 512], P('expert', 'dp')
- grad_up: float32 [32, 1024, 512], P('expert', 'dp')
- grad_down: float32 [32, 512, 1024], P('expert', None, 'dp')
- new_res_gate: bfloat16 [8, 32, 1024, 512], P('dp', 'expert')
- new_res_up: bfloat16 [8, 32, 1024, 512], P('dp', 'expert')
- new_res_down: bfloat16 [8, 32, 512, 1024], P('dp', 'expert')
Inputs may be any that keep to these rules, and one draw needn't show every extreme that they name: `routes`: the 8 entries of a row differ. In the rows of one device (aligned blocks of 256 rows) each expert is named by at most 80 rows, a bound that some block reaches.
All inputs are finite; a program needn't handle non-finite values. Where the computation divides by a largest or mean magnitude, that divisor is 1e-20 or more.
Results may differ from a plain program's by a relative error of at most 0.007.
Values may be sent and summed in bfloat16 or wider, within the bound.
No kernel may reach another device: no remote copies, remote signals or barrier semaphores. Data moves between devices by JAX's collectives and lax.ppermute only.
A program may use at most 192 MiB of HBM per device.

v0:
```python
import functools

import jax
import jax.numpy as jnp
from jax import lax
from jax.experimental import pallas as pl
from jax.experimental.pallas import tpu as pltpu
from jax.sharding import PartitionSpec as P

loss_unscale = 0.0625
epsilon = 1e-05

SIDE = 4
OFFSETS = (0, -1, 1, 2)
CAP = 80
TOK = 256
PACK = TOK + 16
D = 1024
HID = 512
BF = jnp.bfloat16
F32 = jnp.float32
VMEM_LIMIT = 61 * 2**20


def place_of(here):
    core = here[0] & 1
    z, y = here[1] // SIDE, here[1] & (SIDE - 1)
    return here[0] // 2, core, jnp.where(core == 0, z, y), jnp.where(core == 0, y, z)


def expert_at(here, first_off, second_off):
    _, core, first, second = place_of(here)
    first, second = (first + first_off + SIDE) & (SIDE - 1), (second + second_off + SIDE) & (SIDE - 1)
    return jnp.where(core == 0, first * SIDE + second, second * SIDE + first)


def block_place(owner, x, core):
    apart = owner ^ x
    return jnp.where(apart == 0, 0, jnp.where(apart == 1, 2 - core, jnp.where(apart == 2, 3, 1 + core)))


def pairs(axis, step):
    out = []
    for dp in range(8):
        core = dp % 2
        for z in range(SIDE):
            for y in range(SIDE):
                along_z = (axis == 0) == (core == 0)
                z2, y2 = ((z + step) % SIDE, y) if along_z else (z, (y + step) % SIDE)
                out.append((dp * 16 + z * SIDE + y, dp * 16 + z2 * SIDE + y2))
    return out


def hop(value, axis, step):
    return lax.ppermute(value, ("dp", "expert"), pairs(axis, step))


def dp_hop(value, move):
    return lax.ppermute(
        value, "dp", [(x * 2 + c, move(x, c)[0] % SIDE * 2 + move(x, c)[1]) for x in range(SIDE) for c in range(2)]
    )


def nt(left, right):
    return lax.dot_general(left, right, (((1,), (1,)), ((), ())), preferred_element_type=F32)


def pack_kernel(tokens, routes, probs, out):
    out[:TOK, :] = tokens[...]
    weights = probs[...]
    high = weights.astype(BF)
    left = weights - high.astype(F32)
    middle = left.astype(BF)
    low = (left - middle.astype(F32)).astype(BF)
    out[TOK : TOK + 8, :] = jnp.concatenate(
        [routes[...].astype(F32).astype(BF), high, middle, low], axis=1
    )
    out[TOK + 8 :, :] = jnp.zeros((8, D), BF)


def pack(tokens, routes, probs):
    return pl.pallas_call(
        pack_kernel,
        out_shape=jax.ShapeDtypeStruct((PACK, D), BF),
        cost_estimate=pl.CostEstimate(flops=0, bytes_accessed=1_100_000, transcendentals=0),
        name="pack",
    )(tokens, routes.T, probs.T)


def forward_kernel(chained, here, *refs):
    xs, (wg, wu), refs = refs[:8], refs[8:10], refs[10 + (3 if chained else 0) :]
    xt, ht, m12, rows = refs
    for i in range(8):
        rows[i * CAP : (i + 1) * CAP, :] = xs[i][0, 0]
    half = 4 * CAP
    pre = []
    for h in range(2):
        saved = rows[h * half : (h + 1) * half, :]
        pre.append(
            (
                jnp.dot(saved, wg[0], preferred_element_type=F32),
                jnp.dot(saved, wu[0], preferred_element_type=F32),
            )
        )
    xt[0] = rows[...].T
    hidden = []
    for h, (gate, up) in enumerate(pre):
        logistic = jax.nn.sigmoid(gate)
        act = gate * logistic
        m12[0, h * half : (h + 1) * half, :HID] = (up * (logistic * (1.0 + gate * (1.0 - logistic)))).astype(BF)
        m12[0, h * half : (h + 1) * half, HID:] = act.astype(BF)
        hidden.append((act * up).astype(BF))
    ht[0] = jnp.concatenate(hidden, axis=0).T


def forward_terms(e, here, x, wg, wu, carried):
    blocks = x.reshape(2, 16, CAP, D)
    chained = carried is not None

    def block_at(i):
        def at(h, here):
            return e, expert_at(here, OFFSETS[i % 4], h if i < 4 else 3 * h - 1), 0, 0

        return pl.BlockSpec((1, 1, CAP, D), at)

    half = 8 * CAP
    return pl.pallas_call(
        functools.partial(forward_kernel, chained),
        grid_spec=pltpu.PrefetchScalarGridSpec(
            num_scalar_prefetch=1,
            grid=(2,),
            in_specs=[block_at(i) for i in range(8)]
            + [pl.BlockSpec((1, D, HID), lambda h, p: (e, 0, 0))] * 2
            + [pl.BlockSpec(memory_space=pl.ANY)] * (3 if chained else 0),
            out_specs=[
                pl.BlockSpec((1, D, half), lambda h, p: (e, 0, h)),
                pl.BlockSpec((1, HID, half), lambda h, p: (e, 0, h)),
                pl.BlockSpec((1, half, 2 * HID), lambda h, p: (e, h, 0)),
            ],
            scratch_shapes=[pltpu.VMEM((half, D), BF)],
        ),
        out_shape=[
            jax.ShapeDtypeStruct((2, D, 16 * CAP), BF),
            jax.ShapeDtypeStruct((2, HID, 16 * CAP), BF),
            jax.ShapeDtypeStruct((2, 16 * CAP, 2 * HID), BF),
        ],
        input_output_aliases={11 + i: i for i in range(3)} if chained else {},
        compiler_params=pltpu.CompilerParams(vmem_limit_bytes=VMEM_LIMIT),
        cost_estimate=pl.CostEstimate(flops=2_700_000_000, bytes_accessed=15_000_000, transcendentals=655_360),
        name="forward_terms",
    )(here, *([blocks] * 8), wg, wu, *(carried or ()))


def dispatch_kernel(targets, layout, here, *refs):
    blocks, outs, hots = refs[:4], refs[4 : 4 + len(layout)], refs[4 + len(layout) :]
    before = (
        lax.broadcasted_iota(jnp.int32, (TOK, TOK), 0) < lax.broadcasted_iota(jnp.int32, (TOK, TOK), 1)
    ).astype(BF)
    slot = lax.broadcasted_iota(jnp.int32, (CAP, TOK), 0).astype(F32)
    names = [(2 * expert_at(here, 0, OFFSETS[t]) + e).astype(F32) for t in targets for e in range(2)]
    named, weights = [], []
    for i in range(4):
        meta = blocks[i][TOK:, :].astype(F32)[:8]
        routes = meta[:, :TOK]
        probs = meta[:, TOK : 2 * TOK] + meta[:, 2 * TOK : 3 * TOK] + meta[:, 3 * TOK :]
        for name in names:
            hit = routes == name
            named.append(jnp.sum(jnp.where(hit, 1.0, 0.0), axis=0, keepdims=True))
            weights.append(jnp.sum(jnp.where(hit, probs, 0.0), axis=0, keepdims=True))
    mask = jnp.concatenate(named, axis=0)
    rank = jnp.dot(mask.astype(BF), before, preferred_element_type=F32)
    key = jnp.where(mask > 0.5, rank, -1.0)
    per = len(names)
    for i in range(4):
        halves, scales = [], []
        for k in range(per):
            hit = slot == key[per * i + k : per * i + k + 1, :]
            halves.append(jnp.where(hit, 1.0, 0.0).astype(BF))
            scales.append(jnp.sum(jnp.where(hit, weights[per * i + k], 0.0), axis=1, keepdims=True))
            hots[k // 2][i, k % 2 * CAP : (k % 2 + 1) * CAP, :] = halves[k]
        chosen = jnp.concatenate(halves, axis=0)
        taken = jnp.dot(chosen, blocks[i][:TOK, :], preferred_element_type=F32)
        scaled = (taken * jnp.concatenate(scales, axis=0)).astype(BF)
        for out, held in zip(outs, layout):
            for n, (target, e) in enumerate(held):
                k = 2 * targets.index(target) + e
                out[n, i * CAP : (i + 1) * CAP, :] = scaled[k * CAP : (k + 1) * CAP]


def dispatch(targets, layout, here, blocks):
    whole = pl.BlockSpec(memory_space=pltpu.VMEM)
    out = pl.pallas_call(
        functools.partial(dispatch_kernel, targets, layout),
        in_specs=[pl.BlockSpec(memory_space=pltpu.SMEM)] + [whole] * 4,
        out_specs=[whole] * (len(layout) + len(targets)),
        out_shape=[jax.ShapeDtypeStruct((len(held), 4 * CAP, D), BF) for held in layout]
        + [jax.ShapeDtypeStruct((4, 2 * CAP, TOK), BF)] * len(targets),
        compiler_params=pltpu.CompilerParams(vmem_limit_bytes=VMEM_LIMIT),
        cost_estimate=pl.CostEstimate(
            flops=400_000_000 * len(targets), bytes_accessed=6_000_000, transcendentals=0
        ),
        name="dispatch_" + "".join(str(t) for t in targets),
    )(here, *blocks)
    return out[: len(layout)], out[len(layout) :]


class Copies:
    def __init__(self, semaphores):
        self.semaphores, self.started = semaphores, []

    def start(self, source, target):
        copy = pltpu.make_async_copy(source, target, self.semaphores.at[len(self.started)])
        copy.start()
        self.started.append(copy)
        return copy

    def wait(self):
        for copy in self.started:
            copy.wait()


def halves_of(refs, split):
    out = []
    for two in split:
        out.append([refs[0], refs[1]] if two else [refs[0].at[0], refs[0].at[1]])
        refs = refs[2 if two else 1 :]
    return out


def groups_kernel(groups, split, chained, *refs):
    count = len(groups)
    lent = count + sum(split)
    arrived = halves_of(refs[:lent], split)
    m12, wd, wg, wu = refs[lent : lent + 4]
    refs = refs[lent + 4 + (1 if chained else 0) :]
    gab, outs, refs = refs[0], halves_of(refs[1 : 1 + lent], split), refs[1 + lent :]
    m12_v, wd_v, wg_v, wu_v, cot_v, gab_v, rows_v, sem_in, sem_out = refs
    loads, stores, cot_loads, factor_loads = Copies(sem_in), Copies(sem_out), [], []
    load, store = loads.start, stores.start

    down_loads, weight_loads = [], []
    for n, group in enumerate(groups):
        cot_loads.append([load(arrived[n][e], cot_v.at[n, e]) for e in range(2)])
        if n == 0:
            down_loads = [load(wd.at[e], wd_v.at[e]) for e in range(2)]
        factor_loads.append(
            [load(m12.at[e, pl.ds(group * 4 * CAP, 4 * CAP)], m12_v.at[n, e]) for e in range(2)]
        )
        if n == 0:
            weight_loads = [[load(wg.at[e], wg_v.at[e]), load(wu.at[e], wu_v.at[e])] for e in range(2)]
    for n, group in enumerate(groups):
        place = pl.ds(group * 4 * CAP, 4 * CAP)
        for e in range(2):
            cot_loads[n][e].wait()
            if n == 0:
                down_loads[e].wait()
            grad_hidden = nt(cot_v[n, e], wd_v[e])
            factor_loads[n][e].wait()
            gab_v[n, e, :, :HID] = (grad_hidden * m12_v[n, e, :, :HID].astype(F32)).astype(BF)
            gab_v[n, e, :, HID:] = (grad_hidden * m12_v[n, e, :, HID:].astype(F32)).astype(BF)
            store(gab_v.at[n, e], gab.at[e, place])
        for e in range(2):
            if n == 0:
                for item in weight_loads[e]:
                    item.wait()
            rows_v[n, e] = (nt(gab_v[n, e, :, :HID], wg_v[e]) + nt(gab_v[n, e, :, HID:], wu_v[e])).astype(BF)
            store(rows_v.at[n, e], outs[n][e])
    stores.wait()


def groups_pass(groups, arrived, m12, wd, wg, wu, carried):
    chained = carried is not None
    count = len(groups)
    anywhere = pl.BlockSpec(memory_space=pl.ANY)
    slots = jax.ShapeDtypeStruct((2, 16 * CAP, D), BF)
    split = [isinstance(a, tuple) for a in arrived]
    lent = count + sum(split)
    args = [a for two, a in zip(split, arrived) for a in (a if two else (a,))]
    args += [m12, wd, wg, wu] + ([carried] if chained else [])
    row_shapes = []
    for two in split:
        shape = (4 * CAP, D) if two else (2, 4 * CAP, D)
        row_shapes += [jax.ShapeDtypeStruct(shape, BF)] * (2 if two else 1)
    out = pl.pallas_call(
        functools.partial(groups_kernel, groups, split, chained),
        in_specs=[anywhere] * len(args),
        out_specs=[anywhere] * (1 + lent),
        out_shape=[slots] + row_shapes,
        scratch_shapes=[
            pltpu.VMEM((count, 2, 4 * CAP, 2 * HID), BF),
            pltpu.VMEM((2, HID, D), BF),
            pltpu.VMEM((2, D, HID), BF),
            pltpu.VMEM((2, D, HID), BF),
            pltpu.VMEM((count, 2, 4 * CAP, D), BF),
            pltpu.VMEM((count, 2, 4 * CAP, 2 * HID), BF),
            pltpu.VMEM((count, 2, 4 * CAP, D), BF),
            pltpu.SemaphoreType.DMA((6 + 4 * count,)),
            pltpu.SemaphoreType.DMA((4 * count,)),
        ],
        input_output_aliases={lent + 4: 0} if chained else {},
        compiler_params=pltpu.CompilerParams(vmem_limit_bytes=VMEM_LIMIT),
        cost_estimate=pl.CostEstimate(
            flops=2_100_000_000 * count, bytes_accessed=6_000_000 + 9_000_000 * count, transcendentals=0
        ),
        name="groups_" + "".join(str(g) for g in groups),
    )(*args)
    return out[0], out[1:]


def combine_kernel(*refs):
    rows, hots, outs, (rows_v, hots_v, sem_rows, sem_hots) = refs[:5], refs[5:9], refs[9:13], refs[13:]
    rows = halves_of(rows, (False, False, False, True))
    loads = []
    for i in range(4):
        mine = []
        for k in range(4):
            mine.append(
                pltpu.make_async_copy(
                    hots[k].at[i], hots_v.at[i, pl.ds(k * 2 * CAP, 2 * CAP)], sem_hots.at[4 * i + k]
                )
            )
            for e in range(2):
                mine.append(
                    pltpu.make_async_copy(
                        rows[k][e].at[pl.ds(i * CAP, CAP)],
                        rows_v.at[i, pl.ds((2 * k + e) * CAP, CAP)],
                        sem_rows.at[8 * i + 2 * k + e],
                    )
                )
        for item in mine:
            item.start()
        loads.append(mine)
    for i in range(4):
        for item in loads[i]:
            item.wait()
        outs[i][...] = lax.dot_general(
            hots_v[i], rows_v[i], (((0,), (0,)), ((), ())), preferred_element_type=F32
        ).astype(BF)


def combine(rows, hots):
    anywhere = pl.BlockSpec(memory_space=pl.ANY)
    return pl.pallas_call(
        combine_kernel,
        in_specs=[anywhere] * 9,
        out_specs=[pl.BlockSpec(memory_space=pltpu.VMEM)] * 4,
        out_shape=[jax.ShapeDtypeStruct((TOK, D), BF)] * 4,
        scratch_shapes=[
            pltpu.VMEM((4, 8 * CAP, D), BF),
            pltpu.VMEM((4, 8 * CAP, TOK), BF),
            pltpu.SemaphoreType.DMA((32,)),
            pltpu.SemaphoreType.DMA((16,)),
        ],
        compiler_params=pltpu.CompilerParams(vmem_limit_bytes=VMEM_LIMIT),
        cost_estimate=pl.CostEstimate(flops=1_400_000_000, bytes_accessed=9_000_000, transcendentals=0),
        name="combine",
    )(*rows, *hots)


def compress(local_grad, residual):
    carried = local_grad * loss_unscale + residual.astype(F32)
    magnitude = jnp.mean(jnp.abs(carried), axis=-1, keepdims=True) + epsilon
    compressed = (magnitude * jnp.tanh(carried * (1.0 / magnitude))).astype(BF)
    return compressed, (carried - compressed.astype(F32)).astype(BF)


def gate_up_kernel(here, xt, gab, res_gate, res_up, keep, give_gate, give_up, left_gate, left_up, held):
    x, core, _, _ = place_of(here)
    half = pl.program_id(1)
    grads = [jnp.dot(xt[0, u * 256 : (u + 1) * 256], gab[0], preferred_element_type=F32) for u in range(2)]
    for u in range(2):
        rows = slice(u * 256, (u + 1) * 256)
        kept_at = block_place(2 * half + u, x, core)
        given_at = block_place(2 * half + u, x, 1 - core)
        for m, (res, left) in enumerate(((res_gate, left_gate), (res_up, left_up))):
            held[u, m], left[0, rows] = compress(grads[u][:, m * HID : (m + 1) * HID], res[0, rows])
            keep[m, kept_at, 0] = held[u, m, pl.ds(pl.multiple_of(core * 128, 128), 128)]
            give = (give_gate, give_up)[m]
            give[given_at, 0] = held[u, m, pl.ds(pl.multiple_of((1 - core) * 128, 128), 128)]


def gate_up_grads(here, xt, gab, res_gate, res_up):
    tile = pl.BlockSpec((1, HID, HID), lambda e, t, s: (e, t, 0))
    res_shape = jax.ShapeDtypeStruct((2, D, HID), BF)
    keep_shape = jax.ShapeDtypeStruct((2, SIDE, 2, 128, HID), BF)
    give_shape = jax.ShapeDtypeStruct((SIDE, 2, 128, HID), BF)
    return pl.pallas_call(
        gate_up_kernel,
        grid_spec=pltpu.PrefetchScalarGridSpec(
            num_scalar_prefetch=1,
            grid=(2, 2),
            in_specs=[
                pl.BlockSpec((1, 512, 16 * CAP), lambda e, t, s: (e, t, 0)),
                pl.BlockSpec((1, 16 * CAP, 2 * HID), lambda e, t, s: (e, 0, 0)),
                tile,
                tile,
            ],
            out_specs=[pl.BlockSpec((2, SIDE, 1, 128, HID), lambda e, t, s: (0, 0, e, 0, 0))]
            + [pl.BlockSpec((SIDE, 1, 128, HID), lambda e, t, s: (0, e, 0, 0))] * 2
            + [tile, tile],
            scratch_shapes=[pltpu.VMEM((2, 2, 256, HID), BF)],
        ),
        out_shape=[keep_shape, give_shape, give_shape, res_shape, res_shape],
        compiler_params=pltpu.CompilerParams(vmem_limit_bytes=VMEM_LIMIT),
        cost_estimate=pl.CostEstimate(flops=5_400_000_000, bytes_accessed=22_000_000, transcendentals=2_000_000),
        name="gate_up_grads",
    )(here, xt, gab, res_gate, res_up)


def down_kernel(e, chained, here, ht, res, *refs):
    arrived, refs = refs[:4], refs[4 + (3 if chained else 0) :]
    keep, give, left, ht_v, cot_v, res_v, left_v, sent_v, sem_in, sem_out = refs
    x, core, _, _ = place_of(here)
    loads, stores = Copies(sem_in), Copies(sem_out)
    loads.start(ht.at[e], ht_v)
    for g in range(4):
        source = arrived[g] if len(arrived[g].shape) == 2 else arrived[g].at[e]
        loads.start(source, cot_v.at[pl.ds(g * 4 * CAP, 4 * CAP)])
    loads.start(res.at[e], res_v)
    loads.wait()
    for t in range(2):
        rows = pl.ds(t * 256, 256)
        grads = jnp.dot(ht_v[rows], cot_v[...], preferred_element_type=F32)
        compressed, left_v[rows] = compress(grads, res_v[rows])
        stores.start(left_v.at[rows], left.at[e, rows])
        for owner in range(SIDE):
            for c in range(2):
                at = 2 * owner + c
                sent_v[core ^ c, block_place(owner, x, c), rows] = compressed[:, at * 128 : (at + 1) * 128]
    stores.start(sent_v.at[0], keep.at[:, e])
    stores.start(sent_v.at[1], give.at[:, e])
    stores.wait()


def down_grads(e, here, ht, arrived, res, carried):
    anywhere = pl.BlockSpec(memory_space=pl.ANY)
    blocks = jax.ShapeDtypeStruct((SIDE, 2, HID, 128), BF)
    chained = carried is not None
    pieces = [a[e] if isinstance(a, tuple) else a for a in arrived] + (list(carried) if chained else [])
    return pl.pallas_call(
        functools.partial(down_kernel, e, chained),
        in_specs=[pl.BlockSpec(memory_space=pltpu.SMEM)] + [anywhere] * (2 + len(pieces)),
        out_specs=[anywhere] * 3,
        out_shape=[blocks, blocks, jax.ShapeDtypeStruct((2, HID, D), BF)],
        scratch_shapes=[
            pltpu.VMEM((HID, 16 * CAP), BF),
            pltpu.VMEM((16 * CAP, D), BF),
            pltpu.VMEM((HID, D), BF),
            pltpu.VMEM((HID, D), BF),
            pltpu.VMEM((2, SIDE, HID, 128), BF),
            pltpu.SemaphoreType.DMA((6,)),
            pltpu.SemaphoreType.DMA((4,)),
        ],
        input_output_aliases={7 + i: i for i in range(3)} if chained else {},
        compiler_params=pltpu.CompilerParams(vmem_limit_bytes=VMEM_LIMIT),
        cost_estimate=pl.CostEstimate(flops=1_400_000_000, bytes_accessed=7_000_000, transcendentals=500_000),
        name="down_grads",
    )(here, ht, res, *pieces)


def total(*terms):
    out = terms[0].astype(F32)
    for term in terms[1:]:
        out = out + term.astype(F32)
    return out


def add(*terms):
    return total(*terms).astype(BF)


def partner(stage, x, core):
    return x ^ (1 if stage == core else 3)


def halve(passed, nearer, beside):
    first = dp_hop(passed, lambda x, c: (partner(0, x, c), c))
    first, _ = lax.optimization_barrier((first, beside))
    return first, dp_hop(add(*nearer(first)), lambda x, c: (partner(1, x, c), c))


def on_device(x_saved, d_out, routes, probs, w_gate, w_up, w_down, res_gate, res_up, res_down):
    here = jnp.stack([lax.axis_index("dp"), lax.axis_index("expert")]).astype(jnp.int32)

    own = pack(d_out, routes, probs)
    near = (hop(own, 0, 1), hop(own, 0, -1), hop(own, 0, 2))
    terms = forward_terms(0, here, x_saved[0], w_gate, w_up, None)
    near, terms = lax.optimization_barrier((near, terms))
    layout = (((2, 0), (2, 1)), ((1, 0), (1, 1)), ((3, 0),), ((3, 1),))
    (to_plus, to_minus, far_plus, far_minus), (hot1, hot2, hot3) = dispatch((1, 2, 3), layout, here, (own, *near))
    far_plus, far_minus = hop(far_plus[0], 1, 1), hop(far_minus[0], 1, -1)
    group1, group2 = hop(to_plus, 1, 1), hop(to_minus, 1, -1)
    (group0,), (hot0,) = dispatch((0,), (((0, 0), (0, 1)),), here, (own, *near))
    xt, ht, m12 = forward_terms(1, here, x_saved[0], w_gate, w_up, terms)

    run = functools.partial(groups_pass, m12=m12, wd=w_down, wg=w_gate, wu=w_up)
    gab, (rows0,) = run((0,), [group0], carried=None)
    far_plus, far_minus, gab = lax.optimization_barrier((far_plus, far_minus, gab))
    group3 = (hop(far_plus, 1, 1), hop(far_minus, 1, -1))
    gab, (rows1, rows2) = run((1, 2), [group1, group2], carried=gab)
    near_rows = (hop(rows2, 1, 1), hop(rows1, 1, -1))
    gab, (rows3a, rows3b) = run((3,), [group3], carried=gab)
    half_way = (hop(rows3a, 1, 1), hop(rows3b, 1, -1))

    keep, give_gate, give_up, left_gate, left_up = gate_up_grads(here, xt, gab, res_gate[0], res_up[0])
    near_rows, half_way, give_gate, give_up = lax.optimization_barrier((near_rows, half_way, give_gate, give_up))
    got_gate, got_up = (dp_hop(g, lambda x, c: (x, 1 - c)) for g in (give_gate, give_up))
    far_rows = (hop(half_way[0], 1, 1), hop(half_way[1], 1, -1))
    down = functools.partial(
        down_grads, here=here, ht=ht, arrived=(group0, group1, group2, group3), res=res_down[0]
    )
    carried = down(0, carried=None)
    got_gate, got_up, carried = lax.optimization_barrier((got_gate, got_up, carried))
    got = jnp.stack([got_gate, got_up])
    passed = add(keep[:, 2:], got[:, 2:])
    keep_down, give_down, left_down = down(1, carried=carried)
    far_rows, give_down = lax.optimization_barrier((far_rows, give_down))
    got_down = dp_hop(give_down, lambda x, c: (x, 1 - c))
    passed_down = add(keep_down[2:], got_down[2:])

    far_rows, passed_down = lax.optimization_barrier((far_rows, passed_down))
    mine, before, behind, across = combine((rows0, *near_rows, *far_rows), (hot0, hot1, hot2, hot3))
    terms = (mine, hop(behind, 0, 1), hop(before, 0, -1), hop(across, 0, 2))
    first_in, second_in = halve(passed, lambda first: (keep[:, 1], got[:, 1], first[:, 1]), mine)
    first_down, second_down = halve(
        passed_down, lambda first: (keep_down[1], got_down[1], first[1]), mine
    )
    d_tokens, second_in, second_down = lax.optimization_barrier((add(*terms), second_in, second_down))
    mean = [total(keep[m, 0], got[m, 0], first_in[m, 0], second_in[m]) / 8.0 for m in range(2)]
    mean_down = total(keep_down[0], got_down[0], first_down[0], second_down) / 8.0
    return (d_tokens, mean[0], mean[1], mean_down, left_gate[None], left_up[None], left_down[None])


def solution(mesh):
    in_specs = (
        P("dp", "expert", None, None),
        P(("dp", "expert"), None),
        P(("dp", "expert"), None),
        P(("dp", "expert"), None),
        P("expert", None, None),
        P("expert", None, None),
        P("expert", None, None),
        P("dp", "expert", None, None),
        P("dp", "expert", None, None),
        P("dp", "expert", None, None),
    )
    out_specs = (
        P(("dp", "expert"), None),
        P("expert", "dp", None),
        P("expert", "dp", None),
        P("expert", None, "dp"),
        P("dp", "expert", None, None),
        P("dp", "expert", None, None),
        P("dp", "expert", None, None),
    )
    return jax.shard_map(
        on_device, mesh=mesh, in_specs=in_specs, out_specs=out_specs, check_vma=False
    )
```

profile of v0, /device:TPU:0, one launch (start us, length us, event | category | flops | bytes accessed | tf_op | source)
XLA Modules:
  0.0 149.7 jit_solution(13476490283582634147)
XLA Ops:
  0.6 1.9 %pack.1.refs_0_ = bf16[272,1024]{1,0:T(8,128)(2,1)} custom-call(bf16[256,1024]{1,0:T(8,128)(2,1)} %tokens.1, s32[8,256]{1,0:T(8,128)} %bitcast.65, f32[8,256]{1,0:T(8,128)} %bitcast.66), custom_call_target="tpu_custom_call" | custom-call | bytes 1100000 | tf_op jit(solution)/shard_map/pack/pallas_call | solution.py:82
  2.6 4.0 %collective-permute-start.2 = (bf16[272,1024]{1,0:T(8,128)(2,1)}, bf16[272,1024]{1,0:T(8,128)(2,1)S(1)}, u32[]{:S(2)}, u32[]{:S(2)}) collective-permute-start(bf16[272,1024]{1,0:T(8,128)(2,1)} %pack.1.refs_0_), channel_id=1, source_target_pairs={{0,8},{1,9},{2,10},{3,11},{4,12},{5,13},{6,14},{7,15},{8,0},{9,1},... | collective-permute-start | bytes 1671176 | tf_op jit(solution)/shard_map/ppermute | solution.py:55
  9.1 7.9 %forward_terms.2 = (bf16[2,1024,1280]{2,1,0:T(8,128)(2,1)}, bf16[2,512,1280]{2,1,0:T(8,128)(2,1)}, bf16[2,1280,1024]{2,1,0:T(8,128)(2,1)}) custom-call(s32[2]{0:T(128)} %pad_add_fusion.here, bf16[2,16,80,1024]{3,2,1,0:T(8,128)(2,1)} %bitcast.40, bf16[2,16,80,1024]{3,2,1,0:T(8,128)(2,1)} %bitcast.41, bf16[2,16,80,1024]{3,2,1,0:T(8,128)(2,1)} %bitcast.42, ...), custom_call_target="tpu_custom_call" | custom-call | flops 2700000000 | bytes 15000000 | tf_op jit(solution)/shard_map/forward_terms/pallas_call | solution.py:127
  17.0 4.2 %collective-permute-done.1.refs_2_ = bf16[272,1024]{1,0:T(8,128)(2,1)S(1)} collective-permute-done((bf16[272,1024]{1,0:T(8,128)(2,1)}, bf16[272,1024]{1,0:T(8,128)(2,1)S(1)}, u32[]{:S(2)}, u32[]{:S(2)}) %collective-permute-start.1) | collective-permute-done | bytes 557088 | tf_op jit(solution)/shard_map/ppermute | solution.py:55
  22.3 5.3 %dispatch_123.1 = (bf16[2,320,1024]{2,1,0:T(8,128)(2,1)}, bf16[2,320,1024]{2,1,0:T(8,128)(2,1)}, bf16[1,320,1024]{2,1,0:T(8,128)(2,1)}, bf16[1,320,1024]{2,1,0:T...) custom-call(s32[2]{0:T(128)} %pad_add_fusion.here, ...), custom_call_target="tpu_custom_call" | custom-call | flops 1200000000 | bytes 6000000 | tf_op jit(solution)/shard_map/dispatch_123/pallas_call | solution.py:192
  27.6 1.6 %collective-permute-start.3 = (bf16[2,320,1024]{2,1,0:T(8,128)(2,1)}, bf16[2,320,1024]{2,1,0:T(8,128)(2,1)S(1)}, u32[]{:S(2)}, u32[]{:S(2)}) collective-permute-start(bf16[2,320,1024]{2,1,0:T(8,128)(2,1)} %get-tuple-element.88), channel_id=1, source_target_pairs={{0,1},{1,2},{2,3},{3,0},{4,5},{5,6},{6,7},{7,4},{8,9},{9,10},{10,1... | collective-permute-start | bytes 3932168 | tf_op jit(solution)/shard_map/ppermute | solution.py:55
  29.2 1.7 %collective-permute-start.4 = (bf16[2,320,1024]{2,1,0:T(8,128)(2,1)}, bf16[2,320,1024]{2,1,0:T(8,128)(2,1)S(1)}, u32[]{:S(2)}, u32[]{:S(2)}) collective-permute-start(bf16[2,320,1024]{2,1,0:T(8,128)(2,1)} %get-tuple-element.89), channel_id=1, source_target_pairs={{0,3},{1,0},{2,1},{3,2},{4,7},{5,4},{6,5},{7,6},{8,11},{9,8},{10,9... | collective-permute-start | bytes 3932168 | tf_op jit(solution)/shard_map/ppermute | solution.py:55
  31.2 2.9 %collective-permute-start.6 = (bf16[320,1024]{1,0:T(8,128)(2,1)}, bf16[320,1024]{1,0:T(8,128)(2,1)}, u32[]{:S(2)}, u32[]{:S(2)}) collective-permute-start(bf16[320,1024]{1,0:T(8,128)(2,1)} %bitcast.69), channel_id=1, source_target_pairs={{0,3},{1,0},{2,1},{3,2},{4,7},{5,4},{6,5},{7,6},{8,11},{9,8},{10,9... | collective-permute-start | bytes 1966088 | tf_op jit(solution)/shard_map/ppermute | solution.py:55
  34.1 3.4 %dispatch_0.1 = (bf16[2,320,1024]{2,1,0:T(8,128)(2,1)}, bf16[4,160,256]{2,1,0:T(8,128)(2,1)}) custom-call(s32[2]{0:T(128)} %pad_add_fusion.here, bf16[272,1024]{1,0:T(8,128)(2,1)} %pack.1.refs_0_, bf16[272,1024]{1,0:T(8,128)(2,1)} %copy-done.11, bf16[272,1024]{1,0:T(8,128)(2,1)} %copy-done.10, bf16[272,1024]{1,0:T(8,128)(2,1)} %copy-done.9), custom_call_target="tpu_custom_call" | custom-call | flops 400000000 | bytes 6000000 | tf_op jit(solution)/shard_map/dispatch_0/pallas_call | solution.py:192
  37.5 7.9 %forward_terms.3 = (bf16[2,1024,1280]{2,1,0:T(8,128)(2,1)}, bf16[2,512,1280]{2,1,0:T(8,128)(2,1)}, bf16[2,1280,1024]{2,1,0:T(8,128)(2,1)}) custom-call(s32[2]{0:T(128)} %pad_add_fusion.here, bf16[2,16,80,1024]{3,2,1,0:T(8,128)(2,1)} %bitcast.48, bf16[2,16,80,1024]{3,2,1,0:T(8,128)(2,1)} %bitcast.49, ...), custom_call_target="tpu_custom_call", output_to_operand_aliasing={{0}: (11, {}), {1}: (12, {}), {2}: (13, {})} | custom-call | flops 2700000000 | bytes 15000000 | tf_op jit(solution)/shard_map/forward_terms/pallas_call | solution.py:127
  45.3 5.7 %groups_0.1 = (bf16[2,1280,1024]{2,1,0:T(8,128)(2,1)}, bf16[2,320,1024]{2,1,0:T(8,128)(2,1)}) custom-call(bf16[2,320,1024]{2,1,0:T(8,128)(2,1)} %get-tuple-element.82.refs_0_, bf16[2,1280,1024]{2,1,0:T(8,128)(2,1)} %get-tuple-element.86.refs_1_.refs_2_, bf16[2,512,1024]{2,1,0:T(8,128)(2,1)} %refs_3_.5, bf16[2,1024,512]{2,1,0:T(8,128)(2,1)} %refs_4_.5, ...), custom_call_target="tpu_custom_call" | custom-call | flops 2100000000 | bytes 15000000 | tf_op jit(solution)/shard_map/groups_0/pallas_call | solution.py:284
  51.0 2.8 %collective-permute-done.5 = bf16[320,1024]{1,0:T(8,128)(2,1)} collective-permute-done((bf16[320,1024]{1,0:T(8,128)(2,1)}, bf16[320,1024]{1,0:T(8,128)(2,1)}, u32[]{:S(2)}, u32[]{:S(2)}) %collective-permute-start.5) | collective-permute-done | bytes 655392 | tf_op jit(solution)/shard_map/ppermute | solution.py:55
  54.1 1.6 %collective-permute-start.9 = (bf16[320,1024]{1,0:T(8,128)(2,1)}, bf16[320,1024]{1,0:T(8,128)(2,1)}, u32[]{:S(2)}, u32[]{:S(2)}) collective-permute-start(bf16[320,1024]{1,0:T(8,128)(2,1)} %collective-permute-done.5), channel_id=1, source_target_pairs={{0,1},{1,2},{2,3},{3,0},{4,5},{5,6},{6,7},{7,4},{8,9},{9,10},{10,1... | collective-permute-start | bytes 1966088 | tf_op jit(solution)/shard_map/ppermute | solution.py:55
  55.7 1.7 %collective-permute-start.10 = (bf16[320,1024]{1,0:T(8,128)(2,1)}, bf16[320,1024]{1,0:T(8,128)(2,1)}, u32[]{:S(2)}, u32[]{:S(2)}) collective-permute-start(bf16[320,1024]{1,0:T(8,128)(2,1)} %collective-permute-done.6), channel_id=1, source_target_pairs={{0,3},{1,0},{2,1},{3,2},{4,7},{5,4},{6,5},{7,6},{8,11},{9,8},{10,9... | collective-permute-start | bytes 1966088 | tf_op jit(solution)/shard_map/ppermute | solution.py:55
  59.5 8.7 %groups_12.1 = (bf16[2,1280,1024]{2,1,0:T(8,128)(2,1)}, bf16[2,320,1024]{2,1,0:T(8,128)(2,1)}, bf16[2,320,1024]{2,1,0:T(8,128)(2,1)}) custom-call(bf16[2,320,1024]{2,1,0:T(8,128)(2,1)} %copy-done, bf16[2,320,1024]{2,1,0:T(8,128)(2,1)} %copy-done.1, bf16[2,1280,1024]{2,1,0:T(8,128)(2,1)} %get-tuple-element.86.refs_1_.refs_2_, ...), custom_call_target="tpu_custom_call", output_to_operand_aliasing={{0}: (6, {})} | custom-call | flops 4200000000 | bytes 24000000 | tf_op jit(solution)/shard_map/groups_12/pallas_call | solution.py:284
  68.7 2.9 %collective-permute-start.8 = (bf16[2,320,1024]{2,1,0:T(8,128)(2,1)}, bf16[2,320,1024]{2,1,0:T(8,128)(2,1)S(1)}, u32[]{:S(2)}, u32[]{:S(2)}) collective-permute-start(bf16[2,320,1024]{2,1,0:T(8,128)(2,1)} %get-tuple-element.95), channel_id=1, source_target_pairs={{0,3},{1,0},{2,1},{3,2},{4,7},{5,4},{6,5},{7,6},{8,11},{9,8},{10,9... | collective-permute-start | bytes 3932168 | tf_op jit(solution)/shard_map/ppermute | solution.py:55
  71.5 5.7 %groups_3.1 = (bf16[2,1280,1024]{2,1,0:T(8,128)(2,1)}, bf16[320,1024]{1,0:T(8,128)(2,1)}, bf16[320,1024]{1,0:T(8,128)(2,1)}) custom-call(bf16[320,1024]{1,0:T(8,128)(2,1)} %collective-permute-done.9.refs_0_.refs_3_, bf16[320,1024]{1,0:T(8,128)(2,1)} %collective-permute-done.10.refs_1_.refs_3_, ...), custom_call_target="tpu_custom_call", output_to_operand_aliasing={{0}: (6, {})} | custom-call | flops 2100000000 | bytes 15000000 | tf_op jit(solution)/shard_map/groups_3/pallas_call | solution.py:284
  77.3 3.2 %collective-permute-start.12 = (bf16[320,1024]{1,0:T(8,128)(2,1)}, bf16[320,1024]{1,0:T(8,128)(2,1)}, u32[]{:S(2)}, u32[]{:S(2)}) collective-permute-start(bf16[320,1024]{1,0:T(8,128)(2,1)} %get-tuple-element.100), channel_id=1, source_target_pairs={{0,3},{1,0},{2,1},{3,2},{4,7},{5,4},{6,5},{7,6},{8,11},{9,8},{10,9... | collective-permute-start | bytes 1966088 | tf_op jit(solution)/shard_map/ppermute | solution.py:55
  80.5 13.5 %gate_up_grads.1 = (bf16[2,4,2,128,512]{4,3,2,1,0:T(8,128)(2,1)}, bf16[4,2,128,512]{3,2,1,0:T(8,128)(2,1)}, bf16[4,2,128,512]{3,2,1,0:T(8,128)(2,1)}, bf16[2,1024,512]{2,1,0:T(8,128)(2,1)}, bf16[2,1024,512]{2,1,0:T(8,128)(2,1)}) custom-call(s32[2]{0:T(128)} %pad_add_fusion.here, bf16[2,1024,1280]{2,1,0:T(8,128)(2,1)} %get-tuple-element.101.xt, ...), custom_call_target="tpu_custom_call" | custom-call | flops 5400000000 | bytes 22000000 | tf_op jit(solution)/shard_map/gate_up_grads/pallas_call | solution.py:387
  96.9 2.8 %collective-permute-start.14 = (bf16[320,1024]{1,0:T(8,128)(2,1)}, bf16[320,1024]{1,0:T(8,128)(2,1)}, u32[]{:S(2)}, u32[]{:S(2)}) collective-permute-start(bf16[320,1024]{1,0:T(8,128)(2,1)} %collective-permute-done.12), channel_id=1, source_target_pairs={{0,3},{1,0},{2,1},{3,2},{4,7},{5,4},{6,5},{7,6},{8,11},{9,8},{10,9... | collective-permute-start | bytes 1966088 | tf_op jit(solution)/shard_map/ppermute | solution.py:55
  99.7 6.4 %down_grads.2 = (bf16[4,2,512,128]{3,2,1,0:T(8,128)(2,1)}, bf16[4,2,512,128]{3,2,1,0:T(8,128)(2,1)}, bf16[2,512,1024]{2,1,0:T(8,128)(2,1)}) custom-call(s32[2]{0:T(128)} %pad_add_fusion.here, bf16[2,512,1280]{2,1,0:T(8,128)(2,1)} %get-tuple-element.109.ht, bf16[2,512,1024]{2,1,0:T(8,128)(2,1)} %bitcast.56, bf16[2,320,1024]{2,1,0:T(8,128)(2,1)} %get-tuple-element.82.refs_0_, ...), custom_call_target="tpu_custom_call" | custom-call | flops 1400000000 | bytes 7000000 | tf_op jit(solution)/shard_map/down_grads/pallas_call | solution.py:440
  106.1 6.4 %down_grads.3 = (bf16[4,2,512,128]{3,2,1,0:T(8,128)(2,1)}, bf16[4,2,512,128]{3,2,1,0:T(8,128)(2,1)}, bf16[2,512,1024]{2,1,0:T(8,128)(2,1)}) custom-call(s32[2]{0:T(128)} %pad_add_fusion.here, bf16[2,512,1280]{2,1,0:T(8,128)(2,1)} %get-tuple-element.109.ht, ...), custom_call_target="tpu_custom_call", output_to_operand_aliasing={{0}: (7, {}), {1}: (8, {}), {2}: (9, {})} | custom-call | flops 1400000000 | bytes 7000000 | tf_op jit(solution)/shard_map/down_grads/pallas_call | solution.py:440
  112.6 2.7 %add_convert_fusion = bf16[2,2,2,128,512]{4,3,2,0,1:T(8,128)(2,1)} fusion(bf16[1,4,2,128,512]{4,3,2,0,1:T(8,128)(2,1)S(1)} %bitcast.61, bf16[1,4,2,128,512]{4,3,2,0,1:T(8,128)(2,1)S(1)} %bitcast.58, bf16[2,4,2,128,512]{4,3,2,1,0:T(8,128)(2,1)} %get-tuple-element.133), kind=kLoop, calls=%fused_computation | loop fusion | flops 3670016 | bytes 4194304 | tf_op jit(solution)/shard_map/convert_element_type | solution.py:469
  118.4 5.7 %combine.1 = (bf16[256,1024]{1,0:T(8,128)(2,1)}, bf16[256,1024]{1,0:T(8,128)(2,1)}, bf16[256,1024]{1,0:T(8,128)(2,1)}, bf16[256,1024]{1,0:T(8,128)(2,1)}) custom-call(bf16[2,320,1024]{2,1,0:T(8,128)(2,1)} %get-tuple-element.87.refs_0_, bf16[2,320,1024]{2,1,0:T(8,128)(2,1)} %copy-done.4, bf16[2,320,1024]{2,1,0:T(8,128)(2,1)} %copy-done.5, ...), custom_call_target="tpu_custom_call" | custom-call | flops 1400000000 | bytes 9000000 | tf_op jit(solution)/shard_map/combine/pallas_call | solution.py:343
  125.0 2.4 %collective-permute-start.19 = (bf16[256,1024]{1,0:T(8,128)(2,1)}, bf16[256,1024]{1,0:T(8,128)(2,1)S(1)}, u32[]{:S(2)}, u32[]{:S(2)}) collective-permute-start(bf16[256,1024]{1,0:T(8,128)(2,1)} %get-tuple-element.131), channel_id=1, source_target_pairs={{0,12},{1,13},{2,14},{3,15},{4,0},{5,1},{6,2},{7,3},{8,4},{9,5},{1... | collective-permute-start | bytes 1572872 | tf_op jit(solution)/shard_map/ppermute | solution.py:55
  128.4 2.0 %collective-permute-done.21 = bf16[2,2,2,128,512]{4,3,2,0,1:T(8,128)(2,1)} collective-permute-done((bf16[2,2,2,128,512]{4,3,2,0,1:T(8,128)(2,1)}, bf16[2,2,2,128,512]{4,3,2,0,1:T(8,128)(2,1)}, u32[]{:S(2)}, u32[]{:S(2)}) %collective-permute-start.21) | collective-permute-done | bytes 1048608 | tf_op jit(solution)/shard_map/ppermute | solution.py:59
  131.9 2.8 %collective-permute-start.22 = (bf16[2,2,128,512]{3,2,1,0:T(8,128)(2,1)S(1)}, bf16[2,2,128,512]{3,2,1,0:T(8,128)(2,1)S(1)}, u32[]{:S(2)}, u32[]{:S(2)}) collective-permute-start(bf16[2,2,128,512]{3,2,1,0:T(8,128)(2,1)S(1)} %fusion), channel_id=1, source_target_pairs={{0,96},{16,48},{32,64},{48,16},{64,32},{80,112},{96,0},{112,80},{1... | collective-permute-start | bytes 1572872 | tf_op jit(solution)/shard_map/ppermute | solution.py:59
  134.7 1.9 %collective-permute-done.23 = bf16[2,2,512,128]{3,2,1,0:T(8,128)(2,1)} collective-permute-done((bf16[2,2,512,128]{3,2,1,0:T(8,128)(2,1)S(1)}, bf16[2,2,512,128]{3,2,1,0:T(8,128)(2,1)}, u32[]{:S(2)}, u32[]{:S(2)}) %collective-permute-start.23) | collective-permute-done | bytes 524320 | tf_op jit(solution)/shard_map/ppermute | solution.py:59
  137.7 2.8 %collective-permute-start.24 = (bf16[2,512,128]{2,1,0:T(8,128)(2,1)S(1)}, bf16[2,512,128]{2,1,0:T(8,128)(2,1)S(1)}, u32[]{:S(2)}, u32[]{:S(2)}) collective-permute-start(bf16[2,512,128]{2,1,0:T(8,128)(2,1)S(1)} %fusion.5), channel_id=1, source_target_pairs={{0,96},{16,48},{32,64},{48,16},{64,32},{80,112},{96,0},{112,80},{1... | collective-permute-start | bytes 786440 | tf_op jit(solution)/shard_map/ppermute | solution.py:59
  142.4 3.0 %collective-permute-done.24 = bf16[2,512,128]{2,1,0:T(8,128)(2,1)S(1)} collective-permute-done((bf16[2,512,128]{2,1,0:T(8,128)(2,1)S(1)}, bf16[2,512,128]{2,1,0:T(8,128)(2,1)S(1)}, u32[]{:S(2)}, u32[]{:S(2)}) %collective-permute-start.24) | collective-permute-done | bytes 262176 | tf_op jit(solution)/shard_map/ppermute | solution.py:59
  145.4 2.4 %fusion.1 = (f32[2,128,512]{2,1,0:T(8,128)}, f32[2,128,512]{2,1,0:T(8,128)}) fusion(bf16[1,4,2,128,512]{4,3,2,1,0:T(8,128)(2,1)S(1)} %bitcast.63, bf16[2,2,128,512]{3,2,1,0:T(8,128)(2,1)S(1)} %collective-permute-done.22, bf16[2,2,2,128,512]{4,3,2,0,1:T(8,128)(2,1)} %collective-permute-done.21, bf16[2,4,2,128,512]{4,3,2,1,0:T(8,128)(2,1)} %get-tuple-element.133, ...), kind=kLoop, calls=%fused_computation.7 | loop fusion | flops 2097152 | bytes 3145728 | tf_op jit(solution)/shard_map/div | solution.py:529
  147.8 1.9 %fusion.4 = f32[2,512,128]{2,1,0:T(8,128)} fusion(bf16[2,512,128]{2,1,0:T(8,128)(2,1)S(1)} %collective-permute-done.24, bf16[4,2,512,128]{3,2,1,0:T(8,128)(2,1)S(1)} %copy-done.7, bf16[2,2,512,128]{3,2,1,0:T(8,128)(2,1)} %collective-permute-done.23, bf16[4,2,512,128]{3,2,1,0:T(8,128)(2,1)S(1)} %copy-done.3), kind=kLoop, calls=%fused_computation.13 | loop fusion | flops 1048576 | bytes 1572864 | tf_op jit(solution)/shard_map/div | solution.py:530
  (64 shorter events, 19.3 us)
Async XLA Ops:
  2.6 14.5 %collective-permute-start.2 = (bf16[272,1024]{1,0:T(8,128)(2,1)}, bf16[272,1024]{1,0:T(8,128)(2,1)S(1)}, u32[]{:S(2)}, u32[]{:S(2)}) collective-permute-start(bf16[272,1024]{1,0:T(8,128)(2,1)} %pack.1.refs_0_), channel_id=1, source_target_pairs={{0,8},{1,9},{2,10},{3,11},{4,12},{5,13},{6,14},{7,15},{8,0},{9,1},... | collective-permute-start | bytes 1671176 | tf_op jit(solution)/shard_map/ppermute | solution.py:55
  6.5 14.7 %collective-permute-start.1 = (bf16[272,1024]{1,0:T(8,128)(2,1)}, bf16[272,1024]{1,0:T(8,128)(2,1)S(1)}, u32[]{:S(2)}, u32[]{:S(2)}) collective-permute-start(bf16[272,1024]{1,0:T(8,128)(2,1)} %pack.1.refs_0_), channel_id=1, source_target_pairs={{0,12},{1,13},{2,14},{3,15},{4,0},{5,1},{6,2},{7,3},{8,4},{9,5},{1... | collective-permute-start | bytes 1671176 | tf_op jit(solution)/shard_map/ppermute | solution.py:55
  7.2 14.0 %collective-permute-start = (bf16[272,1024]{1,0:T(8,128)(2,1)}, bf16[272,1024]{1,0:T(8,128)(2,1)S(1)}, u32[]{:S(2)}, u32[]{:S(2)}) collective-permute-start(bf16[272,1024]{1,0:T(8,128)(2,1)} %pack.1.refs_0_), channel_id=1, source_target_pairs={{0,4},{1,5},{2,6},{3,7},{4,8},{5,9},{6,10},{7,11},{8,12},{9,13},{1... | collective-permute-start | bytes 1671176 | tf_op jit(solution)/shard_map/ppermute | solution.py:55
  17.0 4.2 %copy-start.9 = (bf16[272,1024]{1,0:T(8,128)(2,1)}, bf16[272,1024]{1,0:T(8,128)(2,1)S(1)}, u32[]{:S(2)}) copy-start(bf16[272,1024]{1,0:T(8,128)(2,1)S(1)} %collective-permute-done.2.refs_3_) | copy-start | bytes 1671172
  27.6 29.8 %collective-permute-start.3 = (bf16[2,320,1024]{2,1,0:T(8,128)(2,1)}, bf16[2,320,1024]{2,1,0:T(8,128)(2,1)S(1)}, u32[]{:S(2)}, u32[]{:S(2)}) collective-permute-start(bf16[2,320,1024]{2,1,0:T(8,128)(2,1)} %get-tuple-element.88), channel_id=1, source_target_pairs={{0,1},{1,2},{2,3},{3,0},{4,5},{5,6},{6,7},{7,4},{8,9},{9,10},{10,1... | collective-permute-start | bytes 3932168 | tf_op jit(solution)/shard_map/ppermute | solution.py:55
  29.2 28.2 %collective-permute-start.4 = (bf16[2,320,1024]{2,1,0:T(8,128)(2,1)}, bf16[2,320,1024]{2,1,0:T(8,128)(2,1)S(1)}, u32[]{:S(2)}, u32[]{:S(2)}) collective-permute-start(bf16[2,320,1024]{2,1,0:T(8,128)(2,1)} %get-tuple-element.89), channel_id=1, source_target_pairs={{0,3},{1,0},{2,1},{3,2},{4,7},{5,4},{6,5},{7,6},{8,11},{9,8},{10,9... | collective-permute-start | bytes 3932168 | tf_op jit(solution)/shard_map/ppermute | solution.py:55
  30.9 22.9 %collective-permute-start.5 = (bf16[320,1024]{1,0:T(8,128)(2,1)}, bf16[320,1024]{1,0:T(8,128)(2,1)}, u32[]{:S(2)}, u32[]{:S(2)}) collective-permute-start(bf16[320,1024]{1,0:T(8,128)(2,1)} %bitcast.70), channel_id=1, source_target_pairs={{0,1},{1,2},{2,3},{3,0},{4,5},{5,6},{6,7},{7,4},{8,9},{9,10},{10,1... | collective-permute-start | bytes 1966088 | tf_op jit(solution)/shard_map/ppermute | solution.py:55
  31.2 22.9 %collective-permute-start.6 = (bf16[320,1024]{1,0:T(8,128)(2,1)}, bf16[320,1024]{1,0:T(8,128)(2,1)}, u32[]{:S(2)}, u32[]{:S(2)}) collective-permute-start(bf16[320,1024]{1,0:T(8,128)(2,1)} %bitcast.69), channel_id=1, source_target_pairs={{0,3},{1,0},{2,1},{3,2},{4,7},{5,4},{6,5},{7,6},{8,11},{9,8},{10,9... | collective-permute-start | bytes 1966088 | tf_op jit(solution)/shard_map/ppermute | solution.py:55
  54.1 17.4 %collective-permute-start.9 = (bf16[320,1024]{1,0:T(8,128)(2,1)}, bf16[320,1024]{1,0:T(8,128)(2,1)}, u32[]{:S(2)}, u32[]{:S(2)}) collective-permute-start(bf16[320,1024]{1,0:T(8,128)(2,1)} %collective-permute-done.5), channel_id=1, source_target_pairs={{0,1},{1,2},{2,3},{3,0},{4,5},{5,6},{6,7},{7,4},{8,9},{9,10},{10,1... | collective-permute-start | bytes 1966088 | tf_op jit(solution)/shard_map/ppermute | solution.py:55
  55.7 15.8 %collective-permute-start.10 = (bf16[320,1024]{1,0:T(8,128)(2,1)}, bf16[320,1024]{1,0:T(8,128)(2,1)}, u32[]{:S(2)}, u32[]{:S(2)}) collective-permute-start(bf16[320,1024]{1,0:T(8,128)(2,1)} %collective-permute-done.6), channel_id=1, source_target_pairs={{0,3},{1,0},{2,1},{3,2},{4,7},{5,4},{6,5},{7,6},{8,11},{9,8},{10,9... | collective-permute-start | bytes 1966088 | tf_op jit(solution)/shard_map/ppermute | solution.py:55
  68.2 26.2 %collective-permute-start.7 = (bf16[2,320,1024]{2,1,0:T(8,128)(2,1)}, bf16[2,320,1024]{2,1,0:T(8,128)(2,1)S(1)}, u32[]{:S(2)}, u32[]{:S(2)}) collective-permute-start(bf16[2,320,1024]{2,1,0:T(8,128)(2,1)} %get-tuple-element.94), channel_id=1, source_target_pairs={{0,1},{1,2},{2,3},{3,0},{4,5},{5,6},{6,7},{7,4},{8,9},{9,10},{10,1... | collective-permute-start | bytes 3932168 | tf_op jit(solution)/shard_map/ppermute | solution.py:55
  68.7 25.8 %collective-permute-start.8 = (bf16[2,320,1024]{2,1,0:T(8,128)(2,1)}, bf16[2,320,1024]{2,1,0:T(8,128)(2,1)S(1)}, u32[]{:S(2)}, u32[]{:S(2)}) collective-permute-start(bf16[2,320,1024]{2,1,0:T(8,128)(2,1)} %get-tuple-element.95), channel_id=1, source_target_pairs={{0,3},{1,0},{2,1},{3,2},{4,7},{5,4},{6,5},{7,6},{8,11},{9,8},{10,9... | collective-permute-start | bytes 3932168 | tf_op jit(solution)/shard_map/ppermute | solution.py:55
  77.2 17.2 %collective-permute-start.11 = (bf16[320,1024]{1,0:T(8,128)(2,1)}, bf16[320,1024]{1,0:T(8,128)(2,1)}, u32[]{:S(2)}, u32[]{:S(2)}) collective-permute-start(bf16[320,1024]{1,0:T(8,128)(2,1)} %get-tuple-element.99), channel_id=1, source_target_pairs={{0,1},{1,2},{2,3},{3,0},{4,5},{5,6},{6,7},{7,4},{8,9},{9,10},{10,1... | collective-permute-start | bytes 1966088 | tf_op jit(solution)/shard_map/ppermute | solution.py:55
  77.3 17.2 %collective-permute-start.12 = (bf16[320,1024]{1,0:T(8,128)(2,1)}, bf16[320,1024]{1,0:T(8,128)(2,1)}, u32[]{:S(2)}, u32[]{:S(2)}) collective-permute-start(bf16[320,1024]{1,0:T(8,128)(2,1)} %get-tuple-element.100), channel_id=1, source_target_pairs={{0,3},{1,0},{2,1},{3,2},{4,7},{5,4},{6,5},{7,6},{8,11},{9,8},{10,9... | collective-permute-start | bytes 1966088 | tf_op jit(solution)/shard_map/ppermute | solution.py:55
  94.5 1.5 copy-start.5
  96.0 10.1 %collective-permute-start.15 = (bf16[4,2,128,512]{3,2,1,0:T(8,128)(2,1)}, bf16[4,2,128,512]{3,2,1,0:T(8,128)(2,1)S(1)}, u32[]{:S(2)}, u32[]{:S(2)}) collective-permute-start(bf16[4,2,128,512]{3,2,1,0:T(8,128)(2,1)} %get-tuple-element.110), channel_id=1, source_target_pairs={{0,16},{16,0},{32,48},{48,32},{64,80},{80,64},{96,112},{112,96},{1... | collective-permute-start | bytes 3145736 | tf_op jit(solution)/shard_map/ppermute | solution.py:59
  96.0 10.2 %collective-permute-start.16 = (bf16[4,2,128,512]{3,2,1,0:T(8,128)(2,1)}, bf16[4,2,128,512]{3,2,1,0:T(8,128)(2,1)S(1)}, u32[]{:S(2)}, u32[]{:S(2)}) collective-permute-start(bf16[4,2,128,512]{3,2,1,0:T(8,128)(2,1)} %get-tuple-element.111), channel_id=1, source_target_pairs={{0,16},{16,0},{32,48},{48,32},{64,80},{80,64},{96,112},{112,96},{1... | collective-permute-start | bytes 3145736 | tf_op jit(solution)/shard_map/ppermute | solution.py:59
  96.5 16.0 %collective-permute-start.13 = (bf16[320,1024]{1,0:T(8,128)(2,1)}, bf16[320,1024]{1,0:T(8,128)(2,1)S(1)}, u32[]{:S(2)}, u32[]{:S(2)}) collective-permute-start(bf16[320,1024]{1,0:T(8,128)(2,1)} %collective-permute-done.11), channel_id=1, source_target_pairs={{0,1},{1,2},{2,3},{3,0},{4,5},{5,6},{6,7},{7,4},{8,9},{9,10},{10,1... | collective-permute-start | bytes 1966088 | tf_op jit(solution)/shard_map/ppermute | solution.py:55
  96.9 15.6 %collective-permute-start.14 = (bf16[320,1024]{1,0:T(8,128)(2,1)}, bf16[320,1024]{1,0:T(8,128)(2,1)}, u32[]{:S(2)}, u32[]{:S(2)}) collective-permute-start(bf16[320,1024]{1,0:T(8,128)(2,1)} %collective-permute-done.12), channel_id=1, source_target_pairs={{0,3},{1,0},{2,1},{3,2},{4,7},{5,4},{6,5},{7,6},{8,11},{9,8},{10,9... | collective-permute-start | bytes 1966088 | tf_op jit(solution)/shard_map/ppermute | solution.py:55
  112.5 2.8 %copy-start.8 = (bf16[320,1024]{1,0:T(8,128)(2,1)}, bf16[320,1024]{1,0:T(8,128)(2,1)S(1)}, u32[]{:S(2)}) copy-start(bf16[320,1024]{1,0:T(8,128)(2,1)S(1)} %collective-permute-done.13.refs_3_) | copy-start | bytes 1966084
  112.5 4.3 %collective-permute-start.17 = (bf16[4,2,512,128]{3,2,1,0:T(8,128)(2,1)}, bf16[4,2,512,128]{3,2,1,0:T(8,128)(2,1)S(1)}, u32[]{:S(2)}, u32[]{:S(2)}) collective-permute-start(bf16[4,2,512,128]{3,2,1,0:T(8,128)(2,1)} %get-tuple-element.122), channel_id=1, source_target_pairs={{0,16},{16,0},{32,48},{48,32},{64,80},{80,64},{96,112},{112,96},{1... | collective-permute-start | bytes 3145736 | tf_op jit(solution)/shard_map/ppermute | solution.py:59
  112.6 4.2 %copy-start.2 = (bf16[4,2,512,128]{3,2,1,0:T(8,128)(2,1)S(1)}, bf16[4,2,512,128]{3,2,1,0:T(8,128)(2,1)}, u32[]{:S(2)}) copy-start(bf16[4,2,512,128]{3,2,1,0:T(8,128)(2,1)} %get-tuple-element.121) | copy-start | bytes 3145732
  115.3 15.1 %collective-permute-start.21 = (bf16[2,2,2,128,512]{4,3,2,0,1:T(8,128)(2,1)}, bf16[2,2,2,128,512]{4,3,2,0,1:T(8,128)(2,1)}, u32[]{:S(2)}, u32[]{:S(2)}) collective-permute-start(bf16[2,2,2,128,512]{4,3,2,0,1:T(8,128)(2,1)} %add_convert_fusion), channel_id=1, source_target_pairs={{0,32},{16,112},{32,0},{48,80},{64,96},{80,48},{96,64},{112,16},{1... | collective-permute-start | bytes 3145736 | tf_op jit(solution)/shard_map/ppermute | solution.py:59
  117.8 18.8 %collective-permute-start.23 = (bf16[2,2,512,128]{3,2,1,0:T(8,128)(2,1)S(1)}, bf16[2,2,512,128]{3,2,1,0:T(8,128)(2,1)}, u32[]{:S(2)}, u32[]{:S(2)}) collective-permute-start(bf16[2,2,512,128]{3,2,1,0:T(8,128)(2,1)S(1)} %add_convert_fusion.3), channel_id=1, source_target_pairs={{0,32},{16,112},{32,0},{48,80},{64,96},{80,48},{96,64},{112,16},{1... | collective-permute-start | bytes 1572872 | tf_op jit(solution)/shard_map/ppermute | solution.py:59
  124.1 12.6 %copy-start.3 = (bf16[4,2,512,128]{3,2,1,0:T(8,128)(2,1)S(1)}, bf16[4,2,512,128]{3,2,1,0:T(8,128)(2,1)}, u32[]{:S(2)}) copy-start(bf16[4,2,512,128]{3,2,1,0:T(8,128)(2,1)} %get-tuple-element.121) | copy-start | bytes 3145732
  124.1 12.6 %copy-start.7 = (bf16[4,2,512,128]{3,2,1,0:T(8,128)(2,1)S(1)}, bf16[4,2,512,128]{3,2,1,0:T(8,128)(2,1)}, u32[]{:S(2)}) copy-start(bf16[4,2,512,128]{3,2,1,0:T(8,128)(2,1)} %copy-done.6) | copy-start | bytes 3145732
  124.1 16.5 %collective-permute-start.18 = (bf16[256,1024]{1,0:T(8,128)(2,1)}, bf16[256,1024]{1,0:T(8,128)(2,1)S(1)}, u32[]{:S(2)}, u32[]{:S(2)}) collective-permute-start(bf16[256,1024]{1,0:T(8,128)(2,1)} %get-tuple-element.130), channel_id=1, source_target_pairs={{0,4},{1,5},{2,6},{3,7},{4,8},{5,9},{6,10},{7,11},{8,12},{9,13},{1... | collective-permute-start | bytes 1572872 | tf_op jit(solution)/shard_map/ppermute | solution.py:55
  125.0 15.6 %collective-permute-start.19 = (bf16[256,1024]{1,0:T(8,128)(2,1)}, bf16[256,1024]{1,0:T(8,128)(2,1)S(1)}, u32[]{:S(2)}, u32[]{:S(2)}) collective-permute-start(bf16[256,1024]{1,0:T(8,128)(2,1)} %get-tuple-element.131), channel_id=1, source_target_pairs={{0,12},{1,13},{2,14},{3,15},{4,0},{5,1},{6,2},{7,3},{8,4},{9,5},{1... | collective-permute-start | bytes 1572872 | tf_op jit(solution)/shard_map/ppermute | solution.py:55
  127.4 13.8 %collective-permute-start.20 = (bf16[256,1024]{1,0:T(8,128)(2,1)}, bf16[256,1024]{1,0:T(8,128)(2,1)S(1)}, u32[]{:S(2)}, u32[]{:S(2)}) collective-permute-start(bf16[256,1024]{1,0:T(8,128)(2,1)} %get-tuple-element.132), channel_id=1, source_target_pairs={{0,8},{1,9},{2,10},{3,11},{4,12},{5,13},{6,14},{7,15},{8,0},{9,1},... | collective-permute-start | bytes 1572872 | tf_op jit(solution)/shard_map/ppermute | solution.py:55
  130.4 10.8 %copy-start.12 = (bf16[256,1024]{1,0:T(8,128)(2,1)S(1)}, bf16[256,1024]{1,0:T(8,128)(2,1)}, u32[]{:S(2)}) copy-start(bf16[256,1024]{1,0:T(8,128)(2,1)} %get-tuple-element.129) | copy-start | bytes 1572868
  131.9 10.5 %collective-permute-start.22 = (bf16[2,2,128,512]{3,2,1,0:T(8,128)(2,1)S(1)}, bf16[2,2,128,512]{3,2,1,0:T(8,128)(2,1)S(1)}, u32[]{:S(2)}, u32[]{:S(2)}) collective-permute-start(bf16[2,2,128,512]{3,2,1,0:T(8,128)(2,1)S(1)} %fusion), channel_id=1, source_target_pairs={{0,96},{16,48},{32,64},{48,16},{64,32},{80,112},{96,0},{112,80},{1... | collective-permute-start | bytes 1572872 | tf_op jit(solution)/shard_map/ppermute | solution.py:59
  137.7 7.7 %collective-permute-start.24 = (bf16[2,512,128]{2,1,0:T(8,128)(2,1)S(1)}, bf16[2,512,128]{2,1,0:T(8,128)(2,1)S(1)}, u32[]{:S(2)}, u32[]{:S(2)}) collective-permute-start(bf16[2,512,128]{2,1,0:T(8,128)(2,1)S(1)} %fusion.5), channel_id=1, source_target_pairs={{0,96},{16,48},{32,64},{48,16},{64,32},{80,112},{96,0},{112,80},{1... | collective-permute-start | bytes 786440 | tf_op jit(solution)/shard_map/ppermute | solution.py:59
  (6 other events, 6.1 us)
where the time goes:
time: 150 us
  Pallas kernels  78.3 us (52%)
  starting transfers between devices  38.2 us (25%)
  waiting for transfers between devices  15.5 us (10%)
  other arithmetic  11.4 us (8%)
  local copies, waits for them, and re-layouts  5.54 us (4%)
    ppermute x18, starting transfers between devices, hop(): return lax.ppermute(value, ('dp', 'expert'), pairs(axis, step))  29.9 us
    pallas_call x3, Pallas kernels, groups_pass(): pl.pallas_call(functools.partial(groups_kernel, groups, split, chained),...  20 us
    pallas_call x2, Pallas kernels, forward_terms(): pl.pallas_call(functools.partial(forward_kernel, chained), grid_spec=pltp...  15.7 us
    pallas_call x1, Pallas kernels, gate_up_grads(): pl.pallas_call(gate_up_kernel, grid_spec=pltpu.PrefetchScalarGridSpec(num...  13.5 us
    pallas_call x2, Pallas kernels, down_grads(): pl.pallas_call(functools.partial(down_kernel, e, chained), in_specs=[pl.B...  12.8 us
    pallas_call x2, Pallas kernels, dispatch(): pl.pallas_call(functools.partial(dispatch_kernel, targets, layout), in_sp...  8.74 us
    ppermute x18, waiting for transfers between devices, hop(): return lax.ppermute(value, ('dp', 'expert'), pairs(axis, step))  8.51 us
    ppermute x7, starting transfers between devices, dp_hop(): lax.ppermute(value, 'dp', [(x * 2 + c, move(x, c)[0] % SIDE * 2 + move(x,...  8.29 us
  transfers between devices with their start and end apart: 25, of which 8 were waited for; matrix products, arithmetic and copies ran while one was open for 5% of the time, Pallas kernels for 47%

commit v1 on v0

--- a/solution.py
+++ b/solution.py
@@ -19,7 +19,8 @@
 HID = 512
 BF = jnp.bfloat16
 F32 = jnp.float32
-VMEM_LIMIT = 61 * 2**20
+VMEM_LIMIT = 56 * 2**20
+GROUPS_VMEM_LIMIT = 63 * 2**20
 
 
 def place_of(here):
@@ -298,7 +299,7 @@
             pltpu.SemaphoreType.DMA((4 * count,)),
         ],
         input_output_aliases={lent + 4: 0} if chained else {},
-        compiler_params=pltpu.CompilerParams(vmem_limit_bytes=VMEM_LIMIT),
+        compiler_params=pltpu.CompilerParams(vmem_limit_bytes=GROUPS_VMEM_LIMIT),
         cost_estimate=pl.CostEstimate(
             flops=2_100_000_000 * count, bytes_accessed=6_000_000 + 9_000_000 * count, transcendentals=0
         ),
@@ -407,53 +408,56 @@
     )(here, xt, gab, res_gate, res_up)
 
 
-def down_kernel(e, chained, here, ht, res, *refs):
-    arrived, refs = refs[:4], refs[4 + (3 if chained else 0) :]
-    keep, give, left, ht_v, cot_v, res_v, left_v, sent_v, sem_in, sem_out = refs
+def down_kernel(split, here, ht, res, *refs):
+    lent = 4 + sum(split)
+    arrived, (keep, give, left) = halves_of(refs[:lent], split), refs[lent : lent + 3]
+    ht_v, cot_v, res_v, left_v, sent_v, sem_in, sem_out = refs[lent + 3 :]
     x, core, _, _ = place_of(here)
-    loads, stores = Copies(sem_in), Copies(sem_out)
-    loads.start(ht.at[e], ht_v)
-    for g in range(4):
-        source = arrived[g] if len(arrived[g].shape) == 2 else arrived[g].at[e]
-        loads.start(source, cot_v.at[pl.ds(g * 4 * CAP, 4 * CAP)])
-    loads.start(res.at[e], res_v)
-    loads.wait()
-    for t in range(2):
-        rows = pl.ds(t * 256, 256)
-        grads = jnp.dot(ht_v[rows], cot_v[...], preferred_element_type=F32)
-        compressed, left_v[rows] = compress(grads, res_v[rows])
-        stores.start(left_v.at[rows], left.at[e, rows])
-        for owner in range(SIDE):
-            for c in range(2):
-                at = 2 * owner + c
-                sent_v[core ^ c, block_place(owner, x, c), rows] = compressed[:, at * 128 : (at + 1) * 128]
-    stores.start(sent_v.at[0], keep.at[:, e])
-    stores.start(sent_v.at[1], give.at[:, e])
+    loads, stores, waits = Copies(sem_in), Copies(sem_out), {}
+    for e in range(2):
+        waits[e] = [loads.start(ht.at[e], ht_v.at[e])]
+        waits[e] += [
+            loads.start(arrived[g][e], cot_v.at[e, pl.ds(g * 4 * CAP, 4 * CAP)]) for g in range(4)
+        ]
+        waits[e] += [loads.start(res.at[e], res_v.at[e])]
+    for e in range(2):
+        for item in waits[e]:
+            item.wait()
+        for t in range(2):
+            rows = pl.ds(t * 256, 256)
+            grads = jnp.dot(ht_v[e, rows], cot_v[e], preferred_element_type=F32)
+            compressed, left_v[e, rows] = compress(grads, res_v[e, rows])
+            stores.start(left_v.at[e, rows], left.at[e, rows])
+            for owner in range(SIDE):
+                for c in range(2):
+                    at = 2 * owner + c
+                    sent_v[core ^ c, block_place(owner, x, c), e, rows] = compressed[:, at * 128 : (at + 1) * 128]
+        stores.start(sent_v.at[0, :, e], keep.at[:, e])
+        stores.start(sent_v.at[1, :, e], give.at[:, e])
     stores.wait()
 
 
-def down_grads(e, here, ht, arrived, res, carried):
+def down_grads(here, ht, arrived, res):
     anywhere = pl.BlockSpec(memory_space=pl.ANY)
     blocks = jax.ShapeDtypeStruct((SIDE, 2, HID, 128), BF)
-    chained = carried is not None
-    pieces = [a[e] if isinstance(a, tuple) else a for a in arrived] + (list(carried) if chained else [])
+    split = [isinstance(a, tuple) for a in arrived]
+    pieces = [a for two, one in zip(split, arrived) for a in (one if two else (one,))]
     return pl.pallas_call(
-        functools.partial(down_kernel, e, chained),
+        functools.partial(down_kernel, split),
         in_specs=[pl.BlockSpec(memory_space=pltpu.SMEM)] + [anywhere] * (2 + len(pieces)),
         out_specs=[anywhere] * 3,
         out_shape=[blocks, blocks, jax.ShapeDtypeStruct((2, HID, D), BF)],
         scratch_shapes=[
-            pltpu.VMEM((HID, 16 * CAP), BF),
-            pltpu.VMEM((16 * CAP, D), BF),
-            pltpu.VMEM((HID, D), BF),
-            pltpu.VMEM((HID, D), BF),
-            pltpu.VMEM((2, SIDE, HID, 128), BF),
-            pltpu.SemaphoreType.DMA((6,)),
-            pltpu.SemaphoreType.DMA((4,)),
+            pltpu.VMEM((2, HID, 16 * CAP), BF),
+            pltpu.VMEM((2, 16 * CAP, D), BF),
+            pltpu.VMEM((2, HID, D), BF),
+            pltpu.VMEM((2, HID, D), BF),
+            pltpu.VMEM((2, SIDE, 2, HID, 128), BF),
+            pltpu.SemaphoreType.DMA((12,)),
+            pltpu.SemaphoreType.DMA((8,)),
         ],
-        input_output_aliases={7 + i: i for i in range(3)} if chained else {},
         compiler_params=pltpu.CompilerParams(vmem_limit_bytes=VMEM_LIMIT),
-        cost_estimate=pl.CostEstimate(flops=1_400_000_000, bytes_accessed=7_000_000, transcendentals=500_000),
+        cost_estimate=pl.CostEstimate(flops=2_700_000_000, bytes_accessed=14_000_000, transcendentals=1_000_000),
         name="down_grads",
     )(here, ht, res, *pieces)
 
@@ -506,14 +510,10 @@
     near_rows, half_way, give_gate, give_up = lax.optimization_barrier((near_rows, half_way, give_gate, give_up))
     got_gate, got_up = (dp_hop(g, lambda x, c: (x, 1 - c)) for g in (give_gate, give_up))
     far_rows = (hop(half_way[0], 1, 1), hop(half_way[1], 1, -1))
-    down = functools.partial(
-        down_grads, here=here, ht=ht, arrived=(group0, group1, group2, group3), res=res_down[0]
-    )
-    carried = down(0, carried=None)
-    got_gate, got_up, carried = lax.optimization_barrier((got_gate, got_up, carried))
+    keep_down, give_down, left_down = down_grads(here, ht, (group0, group1, group2, group3), res_down[0])
+    got_gate, got_up, give_down = lax.optimization_barrier((got_gate, got_up, give_down))
     got = jnp.stack([got_gate, got_up])
     passed = add(keep[:, 2:], got[:, 2:])
-    keep_down, give_down, left_down = down(1, carried=carried)
     far_rows, give_down = lax.optimization_barrier((far_rows, give_down))
     got_down = dp_hop(give_down, lambda x, c: (x, 1 - c))
     passed_down = add(keep_down[2:], got_down[2:])

time: 150 us -> 143 us (0.953)
  Pallas kernels: 78.3 us -> 74.1 us
  other arithmetic: 11.4 us -> 7.54 us
  waiting for transfers between devices: 15.5 us -> 19.1 us
  local copies, waits for them, and re-layouts: 5.54 us -> 3.15 us
    ppermute x7, waiting for transfers between devices: 6.97 us -> 11.7 us  [dp_hop(): lax.ppermute(value, 'dp', [(x * 2 + c, move(x, c)[0] % SIDE * 2 + move(x,...]
    pallas_call x2 -> x1, Pallas kernels: 12.8 us -> 8.69 us  [down_grads(): pl.pallas_call(functools.partial(down_kernel, split), in_specs=[pl.BlockS...]
    convert_element_type x5, other arithmetic: 6.48 us -> 3.83 us  [add(): return total(*terms).astype(BF)]
    unnamed x26 -> x20, local copies, waits for them, and re-layouts: 5.54 us -> 3.15 us
  transfers between devices with their start and end apart: 25 -> 25, of which waited for: 8 -> 6; matrix products, arithmetic and copies ran while one was open for 5% -> 3% of each run, Pallas kernels for 47% -> 47%
where the time goes in v1:
time: 143 us
  Pallas kernels  74.1 us (52%)
  starting transfers between devices  38.4 us (27%)
  waiting for transfers between devices  19.1 us (13%)
  other arithmetic  7.54 us (5%)
  local copies, waits for them, and re-layouts  3.15 us (2%)
    ppermute x18, starting transfers between devices, hop(): return lax.ppermute(value, ('dp', 'expert'), pairs(axis, step))  29.8 us
    pallas_call x3, Pallas kernels, groups_pass(): pl.pallas_call(functools.partial(groups_kernel, groups, split, chained),...  19.9 us
    pallas_call x2, Pallas kernels, forward_terms(): pl.pallas_call(functools.partial(forward_kernel, chained), grid_spec=pltp...  15.8 us
    pallas_call x1, Pallas kernels, gate_up_grads(): pl.pallas_call(gate_up_kernel, grid_spec=pltpu.PrefetchScalarGridSpec(num...  13.4 us
    ppermute x7, waiting for transfers between devices, dp_hop(): lax.ppermute(value, 'dp', [(x * 2 + c, move(x, c)[0] % SIDE * 2 + move(x,...  11.7 us
    pallas_call x2, Pallas kernels, dispatch(): pl.pallas_call(functools.partial(dispatch_kernel, targets, layout), in_sp...  8.73 us
    pallas_call x1, Pallas kernels, down_grads(): pl.pallas_call(functools.partial(down_kernel, split), in_specs=[pl.BlockS...  8.69 us
    ppermute x7, starting transfers between devices, dp_hop(): lax.ppermute(value, 'dp', [(x * 2 + c, move(x, c)[0] % SIDE * 2 + move(x,...  8.57 us
  transfers between devices with their start and end apart: 25, of which 6 were waited for; matrix products, arithmetic and copies ran while one was open for 3% of the time, Pallas kernels for 47%

profile of v1, /device:TPU:0, one launch (start us, length us, event | category | flops | bytes accessed | tf_op | source)
XLA Modules:
  0.0 143.1 jit_solution(11351272938287513190)
XLA Ops:
  0.6 1.9 %pack.1.refs_0_ = bf16[272,1024]{1,0:T(8,128)(2,1)} custom-call(bf16[256,1024]{1,0:T(8,128)(2,1)} %tokens.1, s32[8,256]{1,0:T(8,128)} %bitcast.62, f32[8,256]{1,0:T(8,128)} %bitcast.63), custom_call_target="tpu_custom_call" | custom-call | bytes 1100000 | tf_op jit(solution)/shard_map/pack/pallas_call | solution.py:83
  2.6 4.0 %collective-permute-start.2 = (bf16[272,1024]{1,0:T(8,128)(2,1)}, bf16[272,1024]{1,0:T(8,128)(2,1)S(1)}, u32[]{:S(2)}, u32[]{:S(2)}) collective-permute-start(bf16[272,1024]{1,0:T(8,128)(2,1)} %pack.1.refs_0_), channel_id=1, source_target_pairs={{0,8},{1,9},{2,10},{3,11},{4,12},{5,13},{6,14},{7,15},{8,0},{9,1},... | collective-permute-start | bytes 1671176 | tf_op jit(solution)/shard_map/ppermute | solution.py:56
  7.2 1.3 collective-permute-start
  9.1 7.9 %forward_terms.2 = (bf16[2,1024,1280]{2,1,0:T(8,128)(2,1)}, bf16[2,512,1280]{2,1,0:T(8,128)(2,1)}, bf16[2,1280,1024]{2,1,0:T(8,128)(2,1)}) custom-call(s32[2]{0:T(128)} %pad_add_fusion.here, bf16[2,16,80,1024]{3,2,1,0:T(8,128)(2,1)} %bitcast.40, bf16[2,16,80,1024]{3,2,1,0:T(8,128)(2,1)} %bitcast.41, bf16[2,16,80,1024]{3,2,1,0:T(8,128)(2,1)} %bitcast.42, ...), custom_call_target="tpu_custom_call" | custom-call | flops 2700000000 | bytes 15000000 | tf_op jit(solution)/shard_map/forward_terms/pallas_call | solution.py:128
  17.0 4.2 %collective-permute-done.1.refs_2_ = bf16[272,1024]{1,0:T(8,128)(2,1)S(1)} collective-permute-done((bf16[272,1024]{1,0:T(8,128)(2,1)}, bf16[272,1024]{1,0:T(8,128)(2,1)S(1)}, u32[]{:S(2)}, u32[]{:S(2)}) %collective-permute-start.1) | collective-permute-done | bytes 557088 | tf_op jit(solution)/shard_map/ppermute | solution.py:56
  22.3 5.3 %dispatch_123.1 = (bf16[2,320,1024]{2,1,0:T(8,128)(2,1)}, bf16[2,320,1024]{2,1,0:T(8,128)(2,1)}, bf16[1,320,1024]{2,1,0:T(8,128)(2,1)}, bf16[1,320,1024]{2,1,0:T...) custom-call(s32[2]{0:T(128)} %pad_add_fusion.here, ...), custom_call_target="tpu_custom_call" | custom-call | flops 1200000000 | bytes 6000000 | tf_op jit(solution)/shard_map/dispatch_123/pallas_call | solution.py:193
  27.7 1.6 %collective-permute-start.3 = (bf16[2,320,1024]{2,1,0:T(8,128)(2,1)}, bf16[2,320,1024]{2,1,0:T(8,128)(2,1)}, u32[]{:S(2)}, u32[]{:S(2)}) collective-permute-start(bf16[2,320,1024]{2,1,0:T(8,128)(2,1)} %get-tuple-element.83), channel_id=1, source_target_pairs={{0,1},{1,2},{2,3},{3,0},{4,5},{5,6},{6,7},{7,4},{8,9},{9,10},{10,1... | collective-permute-start | bytes 3932168 | tf_op jit(solution)/shard_map/ppermute | solution.py:56
  29.2 1.7 %collective-permute-start.4 = (bf16[2,320,1024]{2,1,0:T(8,128)(2,1)}, bf16[2,320,1024]{2,1,0:T(8,128)(2,1)}, u32[]{:S(2)}, u32[]{:S(2)}) collective-permute-start(bf16[2,320,1024]{2,1,0:T(8,128)(2,1)} %get-tuple-element.84), channel_id=1, source_target_pairs={{0,3},{1,0},{2,1},{3,2},{4,7},{5,4},{6,5},{7,6},{8,11},{9,8},{10,9... | collective-permute-start | bytes 3932168 | tf_op jit(solution)/shard_map/ppermute | solution.py:56
  31.3 2.9 %collective-permute-start.6 = (bf16[320,1024]{1,0:T(8,128)(2,1)}, bf16[320,1024]{1,0:T(8,128)(2,1)}, u32[]{:S(2)}, u32[]{:S(2)}) collective-permute-start(bf16[320,1024]{1,0:T(8,128)(2,1)} %bitcast.67), channel_id=1, source_target_pairs={{0,3},{1,0},{2,1},{3,2},{4,7},{5,4},{6,5},{7,6},{8,11},{9,8},{10,9... | collective-permute-start | bytes 1966088 | tf_op jit(solution)/shard_map/ppermute | solution.py:56
  34.1 3.4 %dispatch_0.1 = (bf16[2,320,1024]{2,1,0:T(8,128)(2,1)}, bf16[4,160,256]{2,1,0:T(8,128)(2,1)}) custom-call(s32[2]{0:T(128)} %pad_add_fusion.here, bf16[272,1024]{1,0:T(8,128)(2,1)} %pack.1.refs_0_, bf16[272,1024]{1,0:T(8,128)(2,1)} %copy-done.7, bf16[272,1024]{1,0:T(8,128)(2,1)} %copy-done.6, bf16[272,1024]{1,0:T(8,128)(2,1)} %copy-done.5), custom_call_target="tpu_custom_call" | custom-call | flops 400000000 | bytes 6000000 | tf_op jit(solution)/shard_map/dispatch_0/pallas_call | solution.py:193
  37.5 7.9 %forward_terms.3 = (bf16[2,1024,1280]{2,1,0:T(8,128)(2,1)}, bf16[2,512,1280]{2,1,0:T(8,128)(2,1)}, bf16[2,1280,1024]{2,1,0:T(8,128)(2,1)}) custom-call(s32[2]{0:T(128)} %pad_add_fusion.here, bf16[2,16,80,1024]{3,2,1,0:T(8,128)(2,1)} %bitcast.48, bf16[2,16,80,1024]{3,2,1,0:T(8,128)(2,1)} %bitcast.49, ...), custom_call_target="tpu_custom_call", output_to_operand_aliasing={{0}: (11, {}), {1}: (12, {}), {2}: (13, {})} | custom-call | flops 2700000000 | bytes 15000000 | tf_op jit(solution)/shard_map/forward_terms/pallas_call | solution.py:128
  45.4 5.7 %groups_0.1 = (bf16[2,1280,1024]{2,1,0:T(8,128)(2,1)}, bf16[2,320,1024]{2,1,0:T(8,128)(2,1)}) custom-call(bf16[2,320,1024]{2,1,0:T(8,128)(2,1)} %get-tuple-element.77.refs_0_, bf16[2,1280,1024]{2,1,0:T(8,128)(2,1)} %get-tuple-element.81.refs_1_.refs_2_, bf16[2,512,1024]{2,1,0:T(8,128)(2,1)} %refs_3_.5, bf16[2,1024,512]{2,1,0:T(8,128)(2,1)} %refs_4_.5, ...), custom_call_target="tpu_custom_call" | custom-call | flops 2100000000 | bytes 15000000 | tf_op jit(solution)/shard_map/groups_0/pallas_call | solution.py:285
  51.1 2.6 %collective-permute-done.5 = bf16[320,1024]{1,0:T(8,128)(2,1)S(1)} collective-permute-done((bf16[320,1024]{1,0:T(8,128)(2,1)}, bf16[320,1024]{1,0:T(8,128)(2,1)S(1)}, u32[]{:S(2)}, u32[]{:S(2)}) %collective-permute-start.5) | collective-permute-done | bytes 655392 | tf_op jit(solution)/shard_map/ppermute | solution.py:56
  55.8 2.0 %collective-permute-start.10 = (bf16[320,1024]{1,0:T(8,128)(2,1)}, bf16[320,1024]{1,0:T(8,128)(2,1)}, u32[]{:S(2)}, u32[]{:S(2)}) collective-permute-start(bf16[320,1024]{1,0:T(8,128)(2,1)} %collective-permute-done.6), channel_id=1, source_target_pairs={{0,3},{1,0},{2,1},{3,2},{4,7},{5,4},{6,5},{7,6},{8,11},{9,8},{10,9... | collective-permute-start | bytes 1966088 | tf_op jit(solution)/shard_map/ppermute | solution.py:56
  57.8 8.5 %groups_12.1 = (bf16[2,1280,1024]{2,1,0:T(8,128)(2,1)}, bf16[2,320,1024]{2,1,0:T(8,128)(2,1)}, bf16[2,320,1024]{2,1,0:T(8,128)(2,1)}) custom-call(bf16[2,320,1024]{2,1,0:T(8,128)(2,1)} %collective-permute-done.3.refs_0_.refs_1_, bf16[2,320,1024]{2,1,0:T(8,128)(2,1)} %collective-permute-done.4.refs_1_.refs_2_, ...), custom_call_target="tpu_custom_call", output_to_operand_aliasing={{0}: (6, {})} | custom-call | flops 4200000000 | bytes 24000000 | tf_op jit(solution)/shard_map/groups_12/pallas_call | solution.py:285
  66.4 3.2 %collective-permute-start.8 = (bf16[2,320,1024]{2,1,0:T(8,128)(2,1)}, bf16[2,320,1024]{2,1,0:T(8,128)(2,1)}, u32[]{:S(2)}, u32[]{:S(2)}) collective-permute-start(bf16[2,320,1024]{2,1,0:T(8,128)(2,1)} %get-tuple-element.90), channel_id=1, source_target_pairs={{0,3},{1,0},{2,1},{3,2},{4,7},{5,4},{6,5},{7,6},{8,11},{9,8},{10,9... | collective-permute-start | bytes 3932168 | tf_op jit(solution)/shard_map/ppermute | solution.py:56
  70.5 5.7 %groups_3.1 = (bf16[2,1280,1024]{2,1,0:T(8,128)(2,1)}, bf16[320,1024]{1,0:T(8,128)(2,1)}, bf16[320,1024]{1,0:T(8,128)(2,1)}) custom-call(bf16[320,1024]{1,0:T(8,128)(2,1)} %copy-done.2, bf16[320,1024]{1,0:T(8,128)(2,1)} %collective-permute-done.10.refs_1_.refs_4_, ...), custom_call_target="tpu_custom_call", output_to_operand_aliasing={{0}: (6, {})} | custom-call | flops 2100000000 | bytes 15000000 | tf_op jit(solution)/shard_map/groups_3/pallas_call | solution.py:285
  76.3 3.2 %collective-permute-start.12 = (bf16[320,1024]{1,0:T(8,128)(2,1)}, bf16[320,1024]{1,0:T(8,128)(2,1)S(1)}, u32[]{:S(2)}, u32[]{:S(2)}) collective-permute-start(bf16[320,1024]{1,0:T(8,128)(2,1)} %get-tuple-element.95), channel_id=1, source_target_pairs={{0,3},{1,0},{2,1},{3,2},{4,7},{5,4},{6,5},{7,6},{8,11},{9,8},{10,9... | collective-permute-start | bytes 1966088 | tf_op jit(solution)/shard_map/ppermute | solution.py:56
  79.5 13.4 %gate_up_grads.1 = (bf16[2,4,2,128,512]{4,3,2,1,0:T(8,128)(2,1)}, bf16[4,2,128,512]{3,2,1,0:T(8,128)(2,1)}, bf16[4,2,128,512]{3,2,1,0:T(8,128)(2,1)}, bf16[2,1024,512]{2,1,0:T(8,128)(2,1)}, bf16[2,1024,512]{2,1,0:T(8,128)(2,1)}) custom-call(s32[2]{0:T(128)} %pad_add_fusion.here, bf16[2,1024,1280]{2,1,0:T(8,128)(2,1)} %get-tuple-element.96.xt, ...), custom_call_target="tpu_custom_call" | custom-call | flops 5400000000 | bytes 22000000 | tf_op jit(solution)/shard_map/gate_up_grads/pallas_call | solution.py:388
  93.6 3.2 %collective-permute-start.14 = (bf16[320,1024]{1,0:T(8,128)(2,1)S(1)}, bf16[320,1024]{1,0:T(8,128)(2,1)S(1)}, u32[]{:S(2)}, u32[]{:S(2)}) collective-permute-start(bf16[320,1024]{1,0:T(8,128)(2,1)S(1)} %collective-permute-done.12), channel_id=1, source_target_pairs={{0,3},{1,0},{2,1},{3,2},{4,7},{5,4},{6,5},{7,6},{8,11},{9,8},{10,9... | collective-permute-start | bytes 1966088 | tf_op jit(solution)/shard_map/ppermute | solution.py:56
  96.8 8.7 %down_grads.1 = (bf16[4,2,512,128]{3,2,1,0:T(8,128)(2,1)}, bf16[4,2,512,128]{3,2,1,0:T(8,128)(2,1)}, bf16[2,512,1024]{2,1,0:T(8,128)(2,1)}) custom-call(s32[2]{0:T(128)} %pad_add_fusion.here, bf16[2,512,1280]{2,1,0:T(8,128)(2,1)} %get-tuple-element.106.ht, bf16[2,512,1024]{2,1,0:T(8,128)(2,1)} %bitcast.66, bf16[2,320,1024]{2,1,0:T(8,128)(2,1)} %get-tuple-element.77.refs_0_, ...), custom_call_target="tpu_custom_call" | custom-call | flops 2700000000 | bytes 14000000 | tf_op jit(solution)/shard_map/down_grads/pallas_call | solution.py:445
  106.5 1.3 add_convert_fusion
  107.8 1.5 %collective-permute-start.21 = (bf16[2,2,2,128,512]{4,3,2,0,1:T(8,128)(2,1)}, bf16[2,2,2,128,512]{4,3,2,0,1:T(8,128)(2,1)S(1)}, u32[]{:S(2)}, u32[]{:S(2)}) collective-permute-start(bf16[2,2,2,128,512]{4,3,2,0,1:T(8,128)(2,1)} %add_convert_fusion), channel_id=1, source_target_pairs={{0,32},{16,112},{32,0},{48,80},{64,96},{80,48},{96,64},{112,16},{1... | collective-permute-start | bytes 3145736 | tf_op jit(solution)/shard_map/ppermute | solution.py:60
  110.3 5.7 %combine.1 = (bf16[256,1024]{1,0:T(8,128)(2,1)}, bf16[256,1024]{1,0:T(8,128)(2,1)}, bf16[256,1024]{1,0:T(8,128)(2,1)}, bf16[256,1024]{1,0:T(8,128)(2,1)}) custom-call(bf16[2,320,1024]{2,1,0:T(8,128)(2,1)} %get-tuple-element.82.refs_0_, bf16[2,320,1024]{2,1,0:T(8,128)(2,1)} %collective-permute-done.7.refs_1_, ...), custom_call_target="tpu_custom_call" | custom-call | flops 1400000000 | bytes 9000000 | tf_op jit(solution)/shard_map/combine/pallas_call | solution.py:344
  116.7 2.5 %collective-permute-start.19 = (bf16[256,1024]{1,0:T(8,128)(2,1)}, bf16[256,1024]{1,0:T(8,128)(2,1)S(1)}, u32[]{:S(2)}, u32[]{:S(2)}) collective-permute-start(bf16[256,1024]{1,0:T(8,128)(2,1)} %get-tuple-element.121), channel_id=1, source_target_pairs={{0,12},{1,13},{2,14},{3,15},{4,0},{5,1},{6,2},{7,3},{8,4},{9,5},{1... | collective-permute-start | bytes 1572872 | tf_op jit(solution)/shard_map/ppermute | solution.py:56
  120.2 2.5 %collective-permute-done.21 = bf16[2,2,2,128,512]{4,3,2,0,1:T(8,128)(2,1)S(1)} collective-permute-done((bf16[2,2,2,128,512]{4,3,2,0,1:T(8,128)(2,1)}, bf16[2,2,2,128,512]{4,3,2,0,1:T(8,128)(2,1)S(1)}, u32[]{:S(2)}, u32[]{:S(2)}) %collective-permute-start.21) | collective-permute-done | bytes 1048608 | tf_op jit(solution)/shard_map/ppermute | solution.py:60
  123.0 2.8 %collective-permute-start.22 = (bf16[2,2,128,512]{3,2,1,0:T(8,128)(2,1)S(1)}, bf16[2,2,128,512]{3,2,1,0:T(8,128)(2,1)S(1)}, u32[]{:S(2)}, u32[]{:S(2)}) collective-permute-start(bf16[2,2,128,512]{3,2,1,0:T(8,128)(2,1)S(1)} %fusion), channel_id=1, source_target_pairs={{0,96},{16,48},{32,64},{48,16},{64,32},{80,112},{96,0},{112,80},{1... | collective-permute-start | bytes 1572872 | tf_op jit(solution)/shard_map/ppermute | solution.py:60
  125.8 5.4 %collective-permute-done.23 = bf16[2,2,512,128]{3,2,1,0:T(8,128)(2,1)} collective-permute-done((bf16[2,2,512,128]{3,2,1,0:T(8,128)(2,1)S(1)}, bf16[2,2,512,128]{3,2,1,0:T(8,128)(2,1)}, u32[]{:S(2)}, u32[]{:S(2)}) %collective-permute-start.23) | collective-permute-done | bytes 524320 | tf_op jit(solution)/shard_map/ppermute | solution.py:60
  132.3 2.7 %collective-permute-start.24 = (bf16[2,512,128]{2,1,0:T(8,128)(2,1)S(1)}, bf16[2,512,128]{2,1,0:T(8,128)(2,1)S(1)}, u32[]{:S(2)}, u32[]{:S(2)}) collective-permute-start(bf16[2,512,128]{2,1,0:T(8,128)(2,1)S(1)} %fusion.5), channel_id=1, source_target_pairs={{0,96},{16,48},{32,64},{48,16},{64,32},{80,112},{96,0},{112,80},{1... | collective-permute-start | bytes 786440 | tf_op jit(solution)/shard_map/ppermute | solution.py:60
  136.2 3.8 %collective-permute-done.24 = bf16[2,512,128]{2,1,0:T(8,128)(2,1)S(1)} collective-permute-done((bf16[2,512,128]{2,1,0:T(8,128)(2,1)S(1)}, bf16[2,512,128]{2,1,0:T(8,128)(2,1)S(1)}, u32[]{:S(2)}, u32[]{:S(2)}) %collective-permute-start.24) | collective-permute-done | bytes 262176 | tf_op jit(solution)/shard_map/ppermute | solution.py:60
  139.9 1.2 fusion.1
  141.2 1.9 %fusion.4 = f32[2,512,128]{2,1,0:T(8,128)} fusion(bf16[2,512,128]{2,1,0:T(8,128)(2,1)S(1)} %collective-permute-done.24, bf16[4,2,512,128]{3,2,1,0:T(8,128)(2,1)S(1)} %collective-permute-done.17, bf16[2,2,512,128]{3,2,1,0:T(8,128)(2,1)} %collective-permute-done.23, bf16[4,2,512,128]{3,2,1,0:T(8,128)(2,1)S(1)} %copy-done.1), kind=kLoop, calls=%fused_computation.13 | loop fusion | flops 1048576 | bytes 1572864 | tf_op jit(solution)/shard_map/div | solution.py:530
  (57 shorter events, 12.6 us)
Async XLA Ops:
  2.6 14.5 %collective-permute-start.2 = (bf16[272,1024]{1,0:T(8,128)(2,1)}, bf16[272,1024]{1,0:T(8,128)(2,1)S(1)}, u32[]{:S(2)}, u32[]{:S(2)}) collective-permute-start(bf16[272,1024]{1,0:T(8,128)(2,1)} %pack.1.refs_0_), channel_id=1, source_target_pairs={{0,8},{1,9},{2,10},{3,11},{4,12},{5,13},{6,14},{7,15},{8,0},{9,1},... | collective-permute-start | bytes 1671176 | tf_op jit(solution)/shard_map/ppermute | solution.py:56
  6.5 14.7 %collective-permute-start.1 = (bf16[272,1024]{1,0:T(8,128)(2,1)}, bf16[272,1024]{1,0:T(8,128)(2,1)S(1)}, u32[]{:S(2)}, u32[]{:S(2)}) collective-permute-start(bf16[272,1024]{1,0:T(8,128)(2,1)} %pack.1.refs_0_), channel_id=1, source_target_pairs={{0,12},{1,13},{2,14},{3,15},{4,0},{5,1},{6,2},{7,3},{8,4},{9,5},{1... | collective-permute-start | bytes 1671176 | tf_op jit(solution)/shard_map/ppermute | solution.py:56
  7.2 14.0 %collective-permute-start = (bf16[272,1024]{1,0:T(8,128)(2,1)}, bf16[272,1024]{1,0:T(8,128)(2,1)S(1)}, u32[]{:S(2)}, u32[]{:S(2)}) collective-permute-start(bf16[272,1024]{1,0:T(8,128)(2,1)} %pack.1.refs_0_), channel_id=1, source_target_pairs={{0,4},{1,5},{2,6},{3,7},{4,8},{5,9},{6,10},{7,11},{8,12},{9,13},{1... | collective-permute-start | bytes 1671176 | tf_op jit(solution)/shard_map/ppermute | solution.py:56
  17.0 4.2 %copy-start.5 = (bf16[272,1024]{1,0:T(8,128)(2,1)}, bf16[272,1024]{1,0:T(8,128)(2,1)S(1)}, u32[]{:S(2)}) copy-start(bf16[272,1024]{1,0:T(8,128)(2,1)S(1)} %collective-permute-done.2.refs_3_) | copy-start | bytes 1671172
  21.3 1.1 copy-start.7
  27.7 30.1 %collective-permute-start.3 = (bf16[2,320,1024]{2,1,0:T(8,128)(2,1)}, bf16[2,320,1024]{2,1,0:T(8,128)(2,1)}, u32[]{:S(2)}, u32[]{:S(2)}) collective-permute-start(bf16[2,320,1024]{2,1,0:T(8,128)(2,1)} %get-tuple-element.83), channel_id=1, source_target_pairs={{0,1},{1,2},{2,3},{3,0},{4,5},{5,6},{6,7},{7,4},{8,9},{9,10},{10,1... | collective-permute-start | bytes 3932168 | tf_op jit(solution)/shard_map/ppermute | solution.py:56
  29.2 28.6 %collective-permute-start.4 = (bf16[2,320,1024]{2,1,0:T(8,128)(2,1)}, bf16[2,320,1024]{2,1,0:T(8,128)(2,1)}, u32[]{:S(2)}, u32[]{:S(2)}) collective-permute-start(bf16[2,320,1024]{2,1,0:T(8,128)(2,1)} %get-tuple-element.84), channel_id=1, source_target_pairs={{0,3},{1,0},{2,1},{3,2},{4,7},{5,4},{6,5},{7,6},{8,11},{9,8},{10,9... | collective-permute-start | bytes 3932168 | tf_op jit(solution)/shard_map/ppermute | solution.py:56
  30.9 22.8 %collective-permute-start.5 = (bf16[320,1024]{1,0:T(8,128)(2,1)}, bf16[320,1024]{1,0:T(8,128)(2,1)S(1)}, u32[]{:S(2)}, u32[]{:S(2)}) collective-permute-start(bf16[320,1024]{1,0:T(8,128)(2,1)} %bitcast.68), channel_id=1, source_target_pairs={{0,1},{1,2},{2,3},{3,0},{4,5},{5,6},{6,7},{7,4},{8,9},{9,10},{10,1... | collective-permute-start | bytes 1966088 | tf_op jit(solution)/shard_map/ppermute | solution.py:56
  31.3 22.9 %collective-permute-start.6 = (bf16[320,1024]{1,0:T(8,128)(2,1)}, bf16[320,1024]{1,0:T(8,128)(2,1)}, u32[]{:S(2)}, u32[]{:S(2)}) collective-permute-start(bf16[320,1024]{1,0:T(8,128)(2,1)} %bitcast.67), channel_id=1, source_target_pairs={{0,3},{1,0},{2,1},{3,2},{4,7},{5,4},{6,5},{7,6},{8,11},{9,8},{10,9... | collective-permute-start | bytes 1966088 | tf_op jit(solution)/shard_map/ppermute | solution.py:56
  54.5 15.1 %collective-permute-start.9 = (bf16[320,1024]{1,0:T(8,128)(2,1)}, bf16[320,1024]{1,0:T(8,128)(2,1)S(1)}, u32[]{:S(2)}, u32[]{:S(2)}) collective-permute-start(bf16[320,1024]{1,0:T(8,128)(2,1)} %copy-done.9), channel_id=1, source_target_pairs={{0,1},{1,2},{2,3},{3,0},{4,5},{5,6},{6,7},{7,4},{8,9},{9,10},{10,1... | collective-permute-start | bytes 1966088 | tf_op jit(solution)/shard_map/ppermute | solution.py:56
  55.8 13.9 %collective-permute-start.10 = (bf16[320,1024]{1,0:T(8,128)(2,1)}, bf16[320,1024]{1,0:T(8,128)(2,1)}, u32[]{:S(2)}, u32[]{:S(2)}) collective-permute-start(bf16[320,1024]{1,0:T(8,128)(2,1)} %collective-permute-done.6), channel_id=1, source_target_pairs={{0,3},{1,0},{2,1},{3,2},{4,7},{5,4},{6,5},{7,6},{8,11},{9,8},{10,9... | collective-permute-start | bytes 1966088 | tf_op jit(solution)/shard_map/ppermute | solution.py:56
  66.3 26.6 %collective-permute-start.7 = (bf16[2,320,1024]{2,1,0:T(8,128)(2,1)}, bf16[2,320,1024]{2,1,0:T(8,128)(2,1)}, u32[]{:S(2)}, u32[]{:S(2)}) collective-permute-start(bf16[2,320,1024]{2,1,0:T(8,128)(2,1)} %get-tuple-element.89), channel_id=1, source_target_pairs={{0,1},{1,2},{2,3},{3,0},{4,5},{5,6},{6,7},{7,4},{8,9},{9,10},{10,1... | collective-permute-start | bytes 3932168 | tf_op jit(solution)/shard_map/ppermute | solution.py:56
  66.4 26.6 %collective-permute-start.8 = (bf16[2,320,1024]{2,1,0:T(8,128)(2,1)}, bf16[2,320,1024]{2,1,0:T(8,128)(2,1)}, u32[]{:S(2)}, u32[]{:S(2)}) collective-permute-start(bf16[2,320,1024]{2,1,0:T(8,128)(2,1)} %get-tuple-element.90), channel_id=1, source_target_pairs={{0,3},{1,0},{2,1},{3,2},{4,7},{5,4},{6,5},{7,6},{8,11},{9,8},{10,9... | collective-permute-start | bytes 3932168 | tf_op jit(solution)/shard_map/ppermute | solution.py:56
  76.2 16.7 %collective-permute-start.11 = (bf16[320,1024]{1,0:T(8,128)(2,1)}, bf16[320,1024]{1,0:T(8,128)(2,1)S(1)}, u32[]{:S(2)}, u32[]{:S(2)}) collective-permute-start(bf16[320,1024]{1,0:T(8,128)(2,1)} %get-tuple-element.94), channel_id=1, source_target_pairs={{0,1},{1,2},{2,3},{3,0},{4,5},{5,6},{6,7},{7,4},{8,9},{9,10},{10,1... | collective-permute-start | bytes 1966088 | tf_op jit(solution)/shard_map/ppermute | solution.py:56
  76.3 16.7 %collective-permute-start.12 = (bf16[320,1024]{1,0:T(8,128)(2,1)}, bf16[320,1024]{1,0:T(8,128)(2,1)S(1)}, u32[]{:S(2)}, u32[]{:S(2)}) collective-permute-start(bf16[320,1024]{1,0:T(8,128)(2,1)} %get-tuple-element.95), channel_id=1, source_target_pairs={{0,3},{1,0},{2,1},{3,2},{4,7},{5,4},{6,5},{7,6},{8,11},{9,8},{10,9... | collective-permute-start | bytes 1966088 | tf_op jit(solution)/shard_map/ppermute | solution.py:56
  93.0 12.5 %collective-permute-start.15 = (bf16[4,2,128,512]{3,2,1,0:T(8,128)(2,1)}, bf16[4,2,128,512]{3,2,1,0:T(8,128)(2,1)S(1)}, u32[]{:S(2)}, u32[]{:S(2)}) collective-permute-start(bf16[4,2,128,512]{3,2,1,0:T(8,128)(2,1)} %get-tuple-element.104), channel_id=1, source_target_pairs={{0,16},{16,0},{32,48},{48,32},{64,80},{80,64},{96,112},{112,96},{1... | collective-permute-start | bytes 3145736 | tf_op jit(solution)/shard_map/ppermute | solution.py:60
  93.1 12.4 %collective-permute-start.16 = (bf16[4,2,128,512]{3,2,1,0:T(8,128)(2,1)}, bf16[4,2,128,512]{3,2,1,0:T(8,128)(2,1)S(1)}, u32[]{:S(2)}, u32[]{:S(2)}) collective-permute-start(bf16[4,2,128,512]{3,2,1,0:T(8,128)(2,1)} %get-tuple-element.105), channel_id=1, source_target_pairs={{0,16},{16,0},{32,48},{48,32},{64,80},{80,64},{96,112},{112,96},{1... | collective-permute-start | bytes 3145736 | tf_op jit(solution)/shard_map/ppermute | solution.py:60
  93.6 12.0 %collective-permute-start.13 = (bf16[320,1024]{1,0:T(8,128)(2,1)S(1)}, bf16[320,1024]{1,0:T(8,128)(2,1)S(1)}, u32[]{:S(2)}, u32[]{:S(2)}) collective-permute-start(bf16[320,1024]{1,0:T(8,128)(2,1)S(1)} %collective-permute-done.11), channel_id=1, source_target_pairs={{0,1},{1,2},{2,3},{3,0},{4,5},{5,6},{6,7},{7,4},{8,9},{9,10},{10,1... | collective-permute-start | bytes 1966088 | tf_op jit(solution)/shard_map/ppermute | solution.py:56
  93.6 12.0 %collective-permute-start.14 = (bf16[320,1024]{1,0:T(8,128)(2,1)S(1)}, bf16[320,1024]{1,0:T(8,128)(2,1)S(1)}, u32[]{:S(2)}, u32[]{:S(2)}) collective-permute-start(bf16[320,1024]{1,0:T(8,128)(2,1)S(1)} %collective-permute-done.12), channel_id=1, source_target_pairs={{0,3},{1,0},{2,1},{3,2},{4,7},{5,4},{6,5},{7,6},{8,11},{9,8},{10,9... | collective-permute-start | bytes 1966088 | tf_op jit(solution)/shard_map/ppermute | solution.py:56
  96.8 9.7 %copy-start = (bf16[2,4,2,128,512]{4,3,2,1,0:T(8,128)(2,1)S(1)}, bf16[2,4,2,128,512]{4,3,2,1,0:T(8,128)(2,1)}, u32[]{:S(2)}) copy-start(bf16[2,4,2,128,512]{4,3,2,1,0:T(8,128)(2,1)} %get-tuple-element.123) | copy-start | bytes 6291460
  105.6 2.2 %copy-start.3 = (bf16[320,1024]{1,0:T(8,128)(2,1)}, bf16[320,1024]{1,0:T(8,128)(2,1)S(1)}, u32[]{:S(2)}) copy-start(bf16[320,1024]{1,0:T(8,128)(2,1)S(1)} %collective-permute-done.13.refs_3_) | copy-start | bytes 1966084
  105.6 0.9 copy-start.4
  105.6 3.7 %collective-permute-start.17 = (bf16[4,2,512,128]{3,2,1,0:T(8,128)(2,1)}, bf16[4,2,512,128]{3,2,1,0:T(8,128)(2,1)S(1)}, u32[]{:S(2)}, u32[]{:S(2)}) collective-permute-start(bf16[4,2,512,128]{3,2,1,0:T(8,128)(2,1)} %get-tuple-element.112), channel_id=1, source_target_pairs={{0,16},{16,0},{32,48},{48,32},{64,80},{80,64},{96,112},{112,96},{1... | collective-permute-start | bytes 3145736 | tf_op jit(solution)/shard_map/ppermute | solution.py:60
  106.5 2.8 %copy-start.1 = (bf16[4,2,512,128]{3,2,1,0:T(8,128)(2,1)S(1)}, bf16[4,2,512,128]{3,2,1,0:T(8,128)(2,1)}, u32[]{:S(2)}) copy-start(bf16[4,2,512,128]{3,2,1,0:T(8,128)(2,1)} %get-tuple-element.111) | copy-start | bytes 3145732
  107.8 15.0 %collective-permute-start.21 = (bf16[2,2,2,128,512]{4,3,2,0,1:T(8,128)(2,1)}, bf16[2,2,2,128,512]{4,3,2,0,1:T(8,128)(2,1)S(1)}, u32[]{:S(2)}, u32[]{:S(2)}) collective-permute-start(bf16[2,2,2,128,512]{4,3,2,0,1:T(8,128)(2,1)} %add_convert_fusion), channel_id=1, source_target_pairs={{0,32},{16,112},{32,0},{48,80},{64,96},{80,48},{96,64},{112,16},{1... | collective-permute-start | bytes 3145736 | tf_op jit(solution)/shard_map/ppermute | solution.py:60
  109.4 21.8 %collective-permute-start.23 = (bf16[2,2,512,128]{3,2,1,0:T(8,128)(2,1)S(1)}, bf16[2,2,512,128]{3,2,1,0:T(8,128)(2,1)}, u32[]{:S(2)}, u32[]{:S(2)}) collective-permute-start(bf16[2,2,512,128]{3,2,1,0:T(8,128)(2,1)S(1)} %add_convert_fusion.3), channel_id=1, source_target_pairs={{0,32},{16,112},{32,0},{48,80},{64,96},{80,48},{96,64},{112,16},{1... | collective-permute-start | bytes 1572872 | tf_op jit(solution)/shard_map/ppermute | solution.py:60
  115.9 19.1 %collective-permute-start.18 = (bf16[256,1024]{1,0:T(8,128)(2,1)}, bf16[256,1024]{1,0:T(8,128)(2,1)S(1)}, u32[]{:S(2)}, u32[]{:S(2)}) collective-permute-start(bf16[256,1024]{1,0:T(8,128)(2,1)} %get-tuple-element.120), channel_id=1, source_target_pairs={{0,4},{1,5},{2,6},{3,7},{4,8},{5,9},{6,10},{7,11},{8,12},{9,13},{1... | collective-permute-start | bytes 1572872 | tf_op jit(solution)/shard_map/ppermute | solution.py:56
  116.7 18.3 %collective-permute-start.19 = (bf16[256,1024]{1,0:T(8,128)(2,1)}, bf16[256,1024]{1,0:T(8,128)(2,1)S(1)}, u32[]{:S(2)}, u32[]{:S(2)}) collective-permute-start(bf16[256,1024]{1,0:T(8,128)(2,1)} %get-tuple-element.121), channel_id=1, source_target_pairs={{0,12},{1,13},{2,14},{3,15},{4,0},{5,1},{6,2},{7,3},{8,4},{9,5},{1... | collective-permute-start | bytes 1572872 | tf_op jit(solution)/shard_map/ppermute | solution.py:56
  119.3 15.8 %collective-permute-start.20 = (bf16[256,1024]{1,0:T(8,128)(2,1)}, bf16[256,1024]{1,0:T(8,128)(2,1)S(1)}, u32[]{:S(2)}, u32[]{:S(2)}) collective-permute-start(bf16[256,1024]{1,0:T(8,128)(2,1)} %get-tuple-element.122), channel_id=1, source_target_pairs={{0,8},{1,9},{2,10},{3,11},{4,12},{5,13},{6,14},{7,15},{8,0},{9,1},... | collective-permute-start | bytes 1572872 | tf_op jit(solution)/shard_map/ppermute | solution.py:56
  122.8 12.2 %copy-start.8 = (bf16[256,1024]{1,0:T(8,128)(2,1)S(1)}, bf16[256,1024]{1,0:T(8,128)(2,1)}, u32[]{:S(2)}) copy-start(bf16[256,1024]{1,0:T(8,128)(2,1)} %get-tuple-element.119) | copy-start | bytes 1572868
  123.0 13.2 %collective-permute-start.22 = (bf16[2,2,128,512]{3,2,1,0:T(8,128)(2,1)S(1)}, bf16[2,2,128,512]{3,2,1,0:T(8,128)(2,1)S(1)}, u32[]{:S(2)}, u32[]{:S(2)}) collective-permute-start(bf16[2,2,128,512]{3,2,1,0:T(8,128)(2,1)S(1)} %fusion), channel_id=1, source_target_pairs={{0,96},{16,48},{32,64},{48,16},{64,32},{80,112},{96,0},{112,80},{1... | collective-permute-start | bytes 1572872 | tf_op jit(solution)/shard_map/ppermute | solution.py:60
  132.3 7.7 %collective-permute-start.24 = (bf16[2,512,128]{2,1,0:T(8,128)(2,1)S(1)}, bf16[2,512,128]{2,1,0:T(8,128)(2,1)S(1)}, u32[]{:S(2)}, u32[]{:S(2)}) collective-permute-start(bf16[2,512,128]{2,1,0:T(8,128)(2,1)S(1)} %fusion.5), channel_id=1, source_target_pairs={{0,96},{16,48},{32,64},{48,16},{64,32},{80,112},{96,0},{112,80},{1... | collective-permute-start | bytes 786440 | tf_op jit(solution)/shard_map/ppermute | solution.py:60
  (3 other events, 2.6 us)

commit v2 on v1

--- a/solution.py
+++ b/solution.py
@@ -511,9 +511,9 @@
     got_gate, got_up = (dp_hop(g, lambda x, c: (x, 1 - c)) for g in (give_gate, give_up))
     far_rows = (hop(half_way[0], 1, 1), hop(half_way[1], 1, -1))
     keep_down, give_down, left_down = down_grads(here, ht, (group0, group1, group2, group3), res_down[0])
-    got_gate, got_up, give_down = lax.optimization_barrier((got_gate, got_up, give_down))
     got = jnp.stack([got_gate, got_up])
     passed = add(keep[:, 2:], got[:, 2:])
+    passed, give_down = lax.optimization_barrier((passed, give_down))
     far_rows, give_down = lax.optimization_barrier((far_rows, give_down))
     got_down = dp_hop(give_down, lambda x, c: (x, 1 - c))
     passed_down = add(keep_down[2:], got_down[2:])
@@ -525,8 +525,9 @@
     first_down, second_down = halve(
         passed_down, lambda first: (keep_down[1], got_down[1], first[1]), mine
     )
-    d_tokens, second_in, second_down = lax.optimization_barrier((add(*terms), second_in, second_down))
+    d_tokens, second_in = lax.optimization_barrier((add(*terms), second_in))
     mean = [total(keep[m, 0], got[m, 0], first_in[m, 0], second_in[m]) / 8.0 for m in range(2)]
+    mean, second_down = lax.optimization_barrier((mean, second_down))
     mean_down = total(keep_down[0], got_down[0], first_down[0], second_down) / 8.0
     return (d_tokens, mean[0], mean[1], mean_down, left_gate[None], left_up[None], left_down[None])
 

time: 143 us -> 141 us (0.986)
  waiting for transfers between devices: 19.1 us -> 16 us
    ppermute x7, waiting for transfers between devices: 11.7 us -> 7.31 us  [dp_hop(): lax.ppermute(value, 'dp', [(x * 2 + c, move(x, c)[0] % SIDE * 2 + move(x,...]
  transfers between devices with their start and end apart: 25 -> 25, of which waited for: 6 -> 8; matrix products, arithmetic and copies ran while one was open for 3% -> 5% of each run, Pallas kernels for 47% -> 48%
where the time goes in v2:
time: 141 us
  Pallas kernels  74.1 us (53%)
  starting transfers between devices  39 us (28%)
  waiting for transfers between devices  16 us (11%)
  other arithmetic  8.36 us (6%)
  local copies, waits for them, and re-layouts  2.3 us (2%)
    ppermute x18, starting transfers between devices, hop(): return lax.ppermute(value, ('dp', 'expert'), pairs(axis, step))  29.8 us
    pallas_call x3, Pallas kernels, groups_pass(): pl.pallas_call(functools.partial(groups_kernel, groups, split, chained),...  19.9 us
    pallas_call x2, Pallas kernels, forward_terms(): pl.pallas_call(functools.partial(forward_kernel, chained), grid_spec=pltp...  15.8 us
    pallas_call x1, Pallas kernels, gate_up_grads(): pl.pallas_call(gate_up_kernel, grid_spec=pltpu.PrefetchScalarGridSpec(num...  13.4 us
    ppermute x7, starting transfers between devices, dp_hop(): lax.ppermute(value, 'dp', [(x * 2 + c, move(x, c)[0] % SIDE * 2 + move(x,...  9.13 us
    pallas_call x2, Pallas kernels, dispatch(): pl.pallas_call(functools.partial(dispatch_kernel, targets, layout), in_sp...  8.73 us
    pallas_call x1, Pallas kernels, down_grads(): pl.pallas_call(functools.partial(down_kernel, split), in_specs=[pl.BlockS...  8.69 us
    ppermute x18, waiting for transfers between devices, hop(): return lax.ppermute(value, ('dp', 'expert'), pairs(axis, step))  8.67 us
  transfers between devices with their start and end apart: 25, of which 8 were waited for; matrix products, arithmetic and copies ran while one was open for 5% of the time, Pallas kernels for 48%

profile of v2, /device:TPU:0, one launch (start us, length us, event | category | flops | bytes accessed | tf_op | source)
XLA Modules:
  0.0 140.5 jit_solution(13733080794601279773)
XLA Ops:
  0.6 1.9 %pack.1.refs_0_ = bf16[272,1024]{1,0:T(8,128)(2,1)} custom-call(bf16[256,1024]{1,0:T(8,128)(2,1)} %tokens.1, s32[8,256]{1,0:T(8,128)} %bitcast.62, f32[8,256]{1,0:T(8,128)} %bitcast.63), custom_call_target="tpu_custom_call" | custom-call | bytes 1100000 | tf_op jit(solution)/shard_map/pack/pallas_call | solution.py:83
  2.6 4.0 %collective-permute-start.2 = (bf16[272,1024]{1,0:T(8,128)(2,1)}, bf16[272,1024]{1,0:T(8,128)(2,1)S(1)}, u32[]{:S(2)}, u32[]{:S(2)}) collective-permute-start(bf16[272,1024]{1,0:T(8,128)(2,1)} %pack.1.refs_0_), channel_id=1, source_target_pairs={{0,8},{1,9},{2,10},{3,11},{4,12},{5,13},{6,14},{7,15},{8,0},{9,1},... | collective-permute-start | bytes 1671176 | tf_op jit(solution)/shard_map/ppermute | solution.py:56
  7.2 1.3 collective-permute-start
  9.1 7.9 %forward_terms.2 = (bf16[2,1024,1280]{2,1,0:T(8,128)(2,1)}, bf16[2,512,1280]{2,1,0:T(8,128)(2,1)}, bf16[2,1280,1024]{2,1,0:T(8,128)(2,1)}) custom-call(s32[2]{0:T(128)} %pad_add_fusion.here, bf16[2,16,80,1024]{3,2,1,0:T(8,128)(2,1)} %bitcast.40, bf16[2,16,80,1024]{3,2,1,0:T(8,128)(2,1)} %bitcast.41, bf16[2,16,80,1024]{3,2,1,0:T(8,128)(2,1)} %bitcast.42, ...), custom_call_target="tpu_custom_call" | custom-call | flops 2700000000 | bytes 15000000 | tf_op jit(solution)/shard_map/forward_terms/pallas_call | solution.py:128
  17.0 4.2 %collective-permute-done.1.refs_2_ = bf16[272,1024]{1,0:T(8,128)(2,1)S(1)} collective-permute-done((bf16[272,1024]{1,0:T(8,128)(2,1)}, bf16[272,1024]{1,0:T(8,128)(2,1)S(1)}, u32[]{:S(2)}, u32[]{:S(2)}) %collective-permute-start.1) | collective-permute-done | bytes 557088 | tf_op jit(solution)/shard_map/ppermute | solution.py:56
  22.3 5.3 %dispatch_123.1 = (bf16[2,320,1024]{2,1,0:T(8,128)(2,1)}, bf16[2,320,1024]{2,1,0:T(8,128)(2,1)}, bf16[1,320,1024]{2,1,0:T(8,128)(2,1)}, bf16[1,320,1024]{2,1,0:T...) custom-call(s32[2]{0:T(128)} %pad_add_fusion.here, ...), custom_call_target="tpu_custom_call" | custom-call | flops 1200000000 | bytes 6000000 | tf_op jit(solution)/shard_map/dispatch_123/pallas_call | solution.py:193
  27.7 1.6 %collective-permute-start.3 = (bf16[2,320,1024]{2,1,0:T(8,128)(2,1)}, bf16[2,320,1024]{2,1,0:T(8,128)(2,1)}, u32[]{:S(2)}, u32[]{:S(2)}) collective-permute-start(bf16[2,320,1024]{2,1,0:T(8,128)(2,1)} %get-tuple-element.84), channel_id=1, source_target_pairs={{0,1},{1,2},{2,3},{3,0},{4,5},{5,6},{6,7},{7,4},{8,9},{9,10},{10,1... | collective-permute-start | bytes 3932168 | tf_op jit(solution)/shard_map/ppermute | solution.py:56
  29.2 1.7 %collective-permute-start.4 = (bf16[2,320,1024]{2,1,0:T(8,128)(2,1)}, bf16[2,320,1024]{2,1,0:T(8,128)(2,1)}, u32[]{:S(2)}, u32[]{:S(2)}) collective-permute-start(bf16[2,320,1024]{2,1,0:T(8,128)(2,1)} %get-tuple-element.85), channel_id=1, source_target_pairs={{0,3},{1,0},{2,1},{3,2},{4,7},{5,4},{6,5},{7,6},{8,11},{9,8},{10,9... | collective-permute-start | bytes 3932168 | tf_op jit(solution)/shard_map/ppermute | solution.py:56
  31.3 2.9 %collective-permute-start.6 = (bf16[320,1024]{1,0:T(8,128)(2,1)}, bf16[320,1024]{1,0:T(8,128)(2,1)}, u32[]{:S(2)}, u32[]{:S(2)}) collective-permute-start(bf16[320,1024]{1,0:T(8,128)(2,1)} %bitcast.67), channel_id=1, source_target_pairs={{0,3},{1,0},{2,1},{3,2},{4,7},{5,4},{6,5},{7,6},{8,11},{9,8},{10,9... | collective-permute-start | bytes 1966088 | tf_op jit(solution)/shard_map/ppermute | solution.py:56
  34.1 3.4 %dispatch_0.1 = (bf16[2,320,1024]{2,1,0:T(8,128)(2,1)}, bf16[4,160,256]{2,1,0:T(8,128)(2,1)}) custom-call(s32[2]{0:T(128)} %pad_add_fusion.here, bf16[272,1024]{1,0:T(8,128)(2,1)} %pack.1.refs_0_, bf16[272,1024]{1,0:T(8,128)(2,1)} %copy-done.6, bf16[272,1024]{1,0:T(8,128)(2,1)} %copy-done.5, bf16[272,1024]{1,0:T(8,128)(2,1)} %copy-done.4), custom_call_target="tpu_custom_call" | custom-call | flops 400000000 | bytes 6000000 | tf_op jit(solution)/shard_map/dispatch_0/pallas_call | solution.py:193
  37.5 7.9 %forward_terms.3 = (bf16[2,1024,1280]{2,1,0:T(8,128)(2,1)}, bf16[2,512,1280]{2,1,0:T(8,128)(2,1)}, bf16[2,1280,1024]{2,1,0:T(8,128)(2,1)}) custom-call(s32[2]{0:T(128)} %pad_add_fusion.here, bf16[2,16,80,1024]{3,2,1,0:T(8,128)(2,1)} %bitcast.48, bf16[2,16,80,1024]{3,2,1,0:T(8,128)(2,1)} %bitcast.49, ...), custom_call_target="tpu_custom_call", output_to_operand_aliasing={{0}: (11, {}), {1}: (12, {}), {2}: (13, {})} | custom-call | flops 2700000000 | bytes 15000000 | tf_op jit(solution)/shard_map/forward_terms/pallas_call | solution.py:128
  45.4 5.7 %groups_0.1 = (bf16[2,1280,1024]{2,1,0:T(8,128)(2,1)}, bf16[2,320,1024]{2,1,0:T(8,128)(2,1)}) custom-call(bf16[2,320,1024]{2,1,0:T(8,128)(2,1)} %get-tuple-element.78.refs_0_, bf16[2,1280,1024]{2,1,0:T(8,128)(2,1)} %get-tuple-element.82.refs_1_.refs_2_, bf16[2,512,1024]{2,1,0:T(8,128)(2,1)} %refs_3_.5, bf16[2,1024,512]{2,1,0:T(8,128)(2,1)} %refs_4_.5, ...), custom_call_target="tpu_custom_call" | custom-call | flops 2100000000 | bytes 15000000 | tf_op jit(solution)/shard_map/groups_0/pallas_call | solution.py:285
  51.1 2.6 %collective-permute-done.5 = bf16[320,1024]{1,0:T(8,128)(2,1)S(1)} collective-permute-done((bf16[320,1024]{1,0:T(8,128)(2,1)}, bf16[320,1024]{1,0:T(8,128)(2,1)S(1)}, u32[]{:S(2)}, u32[]{:S(2)}) %collective-permute-start.5) | collective-permute-done | bytes 655392 | tf_op jit(solution)/shard_map/ppermute | solution.py:56
  55.8 2.0 %collective-permute-start.10 = (bf16[320,1024]{1,0:T(8,128)(2,1)}, bf16[320,1024]{1,0:T(8,128)(2,1)}, u32[]{:S(2)}, u32[]{:S(2)}) collective-permute-start(bf16[320,1024]{1,0:T(8,128)(2,1)} %collective-permute-done.6), channel_id=1, source_target_pairs={{0,3},{1,0},{2,1},{3,2},{4,7},{5,4},{6,5},{7,6},{8,11},{9,8},{10,9... | collective-permute-start | bytes 1966088 | tf_op jit(solution)/shard_map/ppermute | solution.py:56
  57.8 8.5 %groups_12.1 = (bf16[2,1280,1024]{2,1,0:T(8,128)(2,1)}, bf16[2,320,1024]{2,1,0:T(8,128)(2,1)}, bf16[2,320,1024]{2,1,0:T(8,128)(2,1)}) custom-call(bf16[2,320,1024]{2,1,0:T(8,128)(2,1)} %collective-permute-done.3.refs_0_.refs_1_, bf16[2,320,1024]{2,1,0:T(8,128)(2,1)} %collective-permute-done.4.refs_1_.refs_2_, ...), custom_call_target="tpu_custom_call", output_to_operand_aliasing={{0}: (6, {})} | custom-call | flops 4200000000 | bytes 24000000 | tf_op jit(solution)/shard_map/groups_12/pallas_call | solution.py:285
  66.4 3.2 %collective-permute-start.8 = (bf16[2,320,1024]{2,1,0:T(8,128)(2,1)}, bf16[2,320,1024]{2,1,0:T(8,128)(2,1)}, u32[]{:S(2)}, u32[]{:S(2)}) collective-permute-start(bf16[2,320,1024]{2,1,0:T(8,128)(2,1)} %get-tuple-element.91), channel_id=1, source_target_pairs={{0,3},{1,0},{2,1},{3,2},{4,7},{5,4},{6,5},{7,6},{8,11},{9,8},{10,9... | collective-permute-start | bytes 3932168 | tf_op jit(solution)/shard_map/ppermute | solution.py:56
  70.5 5.7 %groups_3.1 = (bf16[2,1280,1024]{2,1,0:T(8,128)(2,1)}, bf16[320,1024]{1,0:T(8,128)(2,1)}, bf16[320,1024]{1,0:T(8,128)(2,1)}) custom-call(bf16[320,1024]{1,0:T(8,128)(2,1)} %copy-done.2, bf16[320,1024]{1,0:T(8,128)(2,1)} %collective-permute-done.10.refs_1_.refs_4_, ...), custom_call_target="tpu_custom_call", output_to_operand_aliasing={{0}: (6, {})} | custom-call | flops 2100000000 | bytes 15000000 | tf_op jit(solution)/shard_map/groups_3/pallas_call | solution.py:285
  76.3 3.2 %collective-permute-start.12 = (bf16[320,1024]{1,0:T(8,128)(2,1)}, bf16[320,1024]{1,0:T(8,128)(2,1)S(1)}, u32[]{:S(2)}, u32[]{:S(2)}) collective-permute-start(bf16[320,1024]{1,0:T(8,128)(2,1)} %get-tuple-element.96), channel_id=1, source_target_pairs={{0,3},{1,0},{2,1},{3,2},{4,7},{5,4},{6,5},{7,6},{8,11},{9,8},{10,9... | collective-permute-start | bytes 1966088 | tf_op jit(solution)/shard_map/ppermute | solution.py:56
  79.5 13.4 %gate_up_grads.1 = (bf16[2,4,2,128,512]{4,3,2,1,0:T(8,128)(2,1)}, bf16[4,2,128,512]{3,2,1,0:T(8,128)(2,1)}, bf16[4,2,128,512]{3,2,1,0:T(8,128)(2,1)}, bf16[2,1024,512]{2,1,0:T(8,128)(2,1)}, bf16[2,1024,512]{2,1,0:T(8,128)(2,1)}) custom-call(s32[2]{0:T(128)} %pad_add_fusion.here, bf16[2,1024,1280]{2,1,0:T(8,128)(2,1)} %get-tuple-element.97.xt, ...), custom_call_target="tpu_custom_call" | custom-call | flops 5400000000 | bytes 22000000 | tf_op jit(solution)/shard_map/gate_up_grads/pallas_call | solution.py:388
  93.5 3.2 %collective-permute-start.14 = (bf16[320,1024]{1,0:T(8,128)(2,1)S(1)}, bf16[320,1024]{1,0:T(8,128)(2,1)}, u32[]{:S(2)}, u32[]{:S(2)}) collective-permute-start(bf16[320,1024]{1,0:T(8,128)(2,1)S(1)} %collective-permute-done.12), channel_id=1, source_target_pairs={{0,3},{1,0},{2,1},{3,2},{4,7},{5,4},{6,5},{7,6},{8,11},{9,8},{10,9... | collective-permute-start | bytes 1966088 | tf_op jit(solution)/shard_map/ppermute | solution.py:56
  96.8 8.7 %down_grads.1 = (bf16[4,2,512,128]{3,2,1,0:T(8,128)(2,1)}, bf16[4,2,512,128]{3,2,1,0:T(8,128)(2,1)}, bf16[2,512,1024]{2,1,0:T(8,128)(2,1)}) custom-call(s32[2]{0:T(128)} %pad_add_fusion.here, bf16[2,512,1280]{2,1,0:T(8,128)(2,1)} %get-tuple-element.108.ht, bf16[2,512,1024]{2,1,0:T(8,128)(2,1)} %bitcast.66, bf16[2,320,1024]{2,1,0:T(8,128)(2,1)} %get-tuple-element.78.refs_0_, ...), custom_call_target="tpu_custom_call" | custom-call | flops 2700000000 | bytes 14000000 | tf_op jit(solution)/shard_map/down_grads/pallas_call | solution.py:445
  105.5 1.3 add_convert_fusion
  106.9 1.6 %collective-permute-start.21 = (bf16[2,2,2,128,512]{4,3,2,0,1:T(8,128)(2,1)}, bf16[2,2,2,128,512]{4,3,2,0,1:T(8,128)(2,1)S(1)}, u32[]{:S(2)}, u32[]{:S(2)}) collective-permute-start(bf16[2,2,2,128,512]{4,3,2,0,1:T(8,128)(2,1)} %add_convert_fusion), channel_id=1, source_target_pairs={{0,32},{16,112},{32,0},{48,80},{64,96},{80,48},{96,64},{112,16},{1... | collective-permute-start | bytes 3145736 | tf_op jit(solution)/shard_map/ppermute | solution.py:60
  110.5 1.5 %collective-permute-start.23 = (bf16[2,2,512,128]{3,2,1,0:T(8,128)(2,1)}, bf16[2,2,512,128]{3,2,1,0:T(8,128)(2,1)}, u32[]{:S(2)}, u32[]{:S(2)}) collective-permute-start(bf16[2,2,512,128]{3,2,1,0:T(8,128)(2,1)} %add_convert_fusion.3), channel_id=1, source_target_pairs={{0,32},{16,112},{32,0},{48,80},{64,96},{80,48},{96,64},{112,16},{1... | collective-permute-start | bytes 1572872 | tf_op jit(solution)/shard_map/ppermute | solution.py:60
  112.0 5.7 %combine.1 = (bf16[256,1024]{1,0:T(8,128)(2,1)}, bf16[256,1024]{1,0:T(8,128)(2,1)}, bf16[256,1024]{1,0:T(8,128)(2,1)}, bf16[256,1024]{1,0:T(8,128)(2,1)}) custom-call(bf16[2,320,1024]{2,1,0:T(8,128)(2,1)} %get-tuple-element.83.refs_0_, bf16[2,320,1024]{2,1,0:T(8,128)(2,1)} %collective-permute-done.7.refs_1_, ...), custom_call_target="tpu_custom_call" | custom-call | flops 1400000000 | bytes 9000000 | tf_op jit(solution)/shard_map/combine/pallas_call | solution.py:344
  118.5 2.5 %collective-permute-start.19 = (bf16[256,1024]{1,0:T(8,128)(2,1)}, bf16[256,1024]{1,0:T(8,128)(2,1)S(1)}, u32[]{:S(2)}, u32[]{:S(2)}) collective-permute-start(bf16[256,1024]{1,0:T(8,128)(2,1)} %get-tuple-element.123), channel_id=1, source_target_pairs={{0,12},{1,13},{2,14},{3,15},{4,0},{5,1},{6,2},{7,3},{8,4},{9,5},{1... | collective-permute-start | bytes 1572872 | tf_op jit(solution)/shard_map/ppermute | solution.py:56
  122.2 2.8 %collective-permute-start.22 = (bf16[2,2,128,512]{3,2,1,0:T(8,128)(2,1)S(1)}, bf16[2,2,128,512]{3,2,1,0:T(8,128)(2,1)S(1)}, u32[]{:S(2)}, u32[]{:S(2)}) collective-permute-start(bf16[2,2,128,512]{3,2,1,0:T(8,128)(2,1)S(1)} %fusion.1), channel_id=1, source_target_pairs={{0,96},{16,48},{32,64},{48,16},{64,32},{80,112},{96,0},{112,80},{1... | collective-permute-start | bytes 1572872 | tf_op jit(solution)/shard_map/ppermute | solution.py:60
  125.1 4.8 %collective-permute-done.23 = bf16[2,2,512,128]{3,2,1,0:T(8,128)(2,1)} collective-permute-done((bf16[2,2,512,128]{3,2,1,0:T(8,128)(2,1)}, bf16[2,2,512,128]{3,2,1,0:T(8,128)(2,1)}, u32[]{:S(2)}, u32[]{:S(2)}) %collective-permute-start.23) | collective-permute-done | bytes 524320 | tf_op jit(solution)/shard_map/ppermute | solution.py:60
  131.0 2.5 %collective-permute-start.24 = (bf16[2,512,128]{2,1,0:T(8,128)(2,1)S(1)}, bf16[2,512,128]{2,1,0:T(8,128)(2,1)S(1)}, u32[]{:S(2)}, u32[]{:S(2)}) collective-permute-start(bf16[2,512,128]{2,1,0:T(8,128)(2,1)S(1)} %fusion.6), channel_id=1, source_target_pairs={{0,96},{16,48},{32,64},{48,16},{64,32},{80,112},{96,0},{112,80},{1... | collective-permute-start | bytes 786440 | tf_op jit(solution)/shard_map/ppermute | solution.py:60
  136.0 1.2 fusion.2
  137.3 1.4 collective-permute-done.24
  138.6 1.9 %fusion.5 = f32[2,512,128]{2,1,0:T(8,128)} fusion(bf16[2,512,128]{2,1,0:T(8,128)(2,1)S(1)} %collective-permute-done.24, bf16[4,2,512,128]{3,2,1,0:T(8,128)(2,1)S(1)} %collective-permute-done.17, bf16[2,2,512,128]{3,2,1,0:T(8,128)(2,1)} %collective-permute-done.23, bf16[4,2,512,128]{3,2,1,0:T(8,128)(2,1)S(1)} %copy-done.1), kind=kLoop, calls=%fused_computation.16 | loop fusion | flops 1048576 | bytes 1572864 | tf_op jit(solution)/shard_map/div | solution.py:531
  (57 shorter events, 14.1 us)
Async XLA Ops:
  2.6 14.5 %collective-permute-start.2 = (bf16[272,1024]{1,0:T(8,128)(2,1)}, bf16[272,1024]{1,0:T(8,128)(2,1)S(1)}, u32[]{:S(2)}, u32[]{:S(2)}) collective-permute-start(bf16[272,1024]{1,0:T(8,128)(2,1)} %pack.1.refs_0_), channel_id=1, source_target_pairs={{0,8},{1,9},{2,10},{3,11},{4,12},{5,13},{6,14},{7,15},{8,0},{9,1},... | collective-permute-start | bytes 1671176 | tf_op jit(solution)/shard_map/ppermute | solution.py:56
  6.5 14.7 %collective-permute-start.1 = (bf16[272,1024]{1,0:T(8,128)(2,1)}, bf16[272,1024]{1,0:T(8,128)(2,1)S(1)}, u32[]{:S(2)}, u32[]{:S(2)}) collective-permute-start(bf16[272,1024]{1,0:T(8,128)(2,1)} %pack.1.refs_0_), channel_id=1, source_target_pairs={{0,12},{1,13},{2,14},{3,15},{4,0},{5,1},{6,2},{7,3},{8,4},{9,5},{1... | collective-permute-start | bytes 1671176 | tf_op jit(solution)/shard_map/ppermute | solution.py:56
  7.2 14.0 %collective-permute-start = (bf16[272,1024]{1,0:T(8,128)(2,1)}, bf16[272,1024]{1,0:T(8,128)(2,1)S(1)}, u32[]{:S(2)}, u32[]{:S(2)}) collective-permute-start(bf16[272,1024]{1,0:T(8,128)(2,1)} %pack.1.refs_0_), channel_id=1, source_target_pairs={{0,4},{1,5},{2,6},{3,7},{4,8},{5,9},{6,10},{7,11},{8,12},{9,13},{1... | collective-permute-start | bytes 1671176 | tf_op jit(solution)/shard_map/ppermute | solution.py:56
  17.0 4.2 %copy-start.4 = (bf16[272,1024]{1,0:T(8,128)(2,1)}, bf16[272,1024]{1,0:T(8,128)(2,1)S(1)}, u32[]{:S(2)}) copy-start(bf16[272,1024]{1,0:T(8,128)(2,1)S(1)} %collective-permute-done.2.refs_3_) | copy-start | bytes 1671172
  21.3 1.1 copy-start.6
  27.7 30.1 %collective-permute-start.3 = (bf16[2,320,1024]{2,1,0:T(8,128)(2,1)}, bf16[2,320,1024]{2,1,0:T(8,128)(2,1)}, u32[]{:S(2)}, u32[]{:S(2)}) collective-permute-start(bf16[2,320,1024]{2,1,0:T(8,128)(2,1)} %get-tuple-element.84), channel_id=1, source_target_pairs={{0,1},{1,2},{2,3},{3,0},{4,5},{5,6},{6,7},{7,4},{8,9},{9,10},{10,1... | collective-permute-start | bytes 3932168 | tf_op jit(solution)/shard_map/ppermute | solution.py:56
  29.2 28.6 %collective-permute-start.4 = (bf16[2,320,1024]{2,1,0:T(8,128)(2,1)}, bf16[2,320,1024]{2,1,0:T(8,128)(2,1)}, u32[]{:S(2)}, u32[]{:S(2)}) collective-permute-start(bf16[2,320,1024]{2,1,0:T(8,128)(2,1)} %get-tuple-element.85), channel_id=1, source_target_pairs={{0,3},{1,0},{2,1},{3,2},{4,7},{5,4},{6,5},{7,6},{8,11},{9,8},{10,9... | collective-permute-start | bytes 3932168 | tf_op jit(solution)/shard_map/ppermute | solution.py:56
  30.9 22.8 %collective-permute-start.5 = (bf16[320,1024]{1,0:T(8,128)(2,1)}, bf16[320,1024]{1,0:T(8,128)(2,1)S(1)}, u32[]{:S(2)}, u32[]{:S(2)}) collective-permute-start(bf16[320,1024]{1,0:T(8,128)(2,1)} %bitcast.68), channel_id=1, source_target_pairs={{0,1},{1,2},{2,3},{3,0},{4,5},{5,6},{6,7},{7,4},{8,9},{9,10},{10,1... | collective-permute-start | bytes 1966088 | tf_op jit(solution)/shard_map/ppermute | solution.py:56
  31.3 22.9 %collective-permute-start.6 = (bf16[320,1024]{1,0:T(8,128)(2,1)}, bf16[320,1024]{1,0:T(8,128)(2,1)}, u32[]{:S(2)}, u32[]{:S(2)}) collective-permute-start(bf16[320,1024]{1,0:T(8,128)(2,1)} %bitcast.67), channel_id=1, source_target_pairs={{0,3},{1,0},{2,1},{3,2},{4,7},{5,4},{6,5},{7,6},{8,11},{9,8},{10,9... | collective-permute-start | bytes 1966088 | tf_op jit(solution)/shard_map/ppermute | solution.py:56
  54.5 15.1 %collective-permute-start.9 = (bf16[320,1024]{1,0:T(8,128)(2,1)}, bf16[320,1024]{1,0:T(8,128)(2,1)S(1)}, u32[]{:S(2)}, u32[]{:S(2)}) collective-permute-start(bf16[320,1024]{1,0:T(8,128)(2,1)} %copy-done.9), channel_id=1, source_target_pairs={{0,1},{1,2},{2,3},{3,0},{4,5},{5,6},{6,7},{7,4},{8,9},{9,10},{10,1... | collective-permute-start | bytes 1966088 | tf_op jit(solution)/shard_map/ppermute | solution.py:56
  55.8 13.9 %collective-permute-start.10 = (bf16[320,1024]{1,0:T(8,128)(2,1)}, bf16[320,1024]{1,0:T(8,128)(2,1)}, u32[]{:S(2)}, u32[]{:S(2)}) collective-permute-start(bf16[320,1024]{1,0:T(8,128)(2,1)} %collective-permute-done.6), channel_id=1, source_target_pairs={{0,3},{1,0},{2,1},{3,2},{4,7},{5,4},{6,5},{7,6},{8,11},{9,8},{10,9... | collective-permute-start | bytes 1966088 | tf_op jit(solution)/shard_map/ppermute | solution.py:56
  66.3 26.6 %collective-permute-start.7 = (bf16[2,320,1024]{2,1,0:T(8,128)(2,1)}, bf16[2,320,1024]{2,1,0:T(8,128)(2,1)}, u32[]{:S(2)}, u32[]{:S(2)}) collective-permute-start(bf16[2,320,1024]{2,1,0:T(8,128)(2,1)} %get-tuple-element.90), channel_id=1, source_target_pairs={{0,1},{1,2},{2,3},{3,0},{4,5},{5,6},{6,7},{7,4},{8,9},{9,10},{10,1... | collective-permute-start | bytes 3932168 | tf_op jit(solution)/shard_map/ppermute | solution.py:56
  66.4 26.5 %collective-permute-start.8 = (bf16[2,320,1024]{2,1,0:T(8,128)(2,1)}, bf16[2,320,1024]{2,1,0:T(8,128)(2,1)}, u32[]{:S(2)}, u32[]{:S(2)}) collective-permute-start(bf16[2,320,1024]{2,1,0:T(8,128)(2,1)} %get-tuple-element.91), channel_id=1, source_target_pairs={{0,3},{1,0},{2,1},{3,2},{4,7},{5,4},{6,5},{7,6},{8,11},{9,8},{10,9... | collective-permute-start | bytes 3932168 | tf_op jit(solution)/shard_map/ppermute | solution.py:56
  76.2 16.7 %collective-permute-start.11 = (bf16[320,1024]{1,0:T(8,128)(2,1)}, bf16[320,1024]{1,0:T(8,128)(2,1)S(1)}, u32[]{:S(2)}, u32[]{:S(2)}) collective-permute-start(bf16[320,1024]{1,0:T(8,128)(2,1)} %get-tuple-element.95), channel_id=1, source_target_pairs={{0,1},{1,2},{2,3},{3,0},{4,5},{5,6},{6,7},{7,4},{8,9},{9,10},{10,1... | collective-permute-start | bytes 1966088 | tf_op jit(solution)/shard_map/ppermute | solution.py:56
  76.3 16.7 %collective-permute-start.12 = (bf16[320,1024]{1,0:T(8,128)(2,1)}, bf16[320,1024]{1,0:T(8,128)(2,1)S(1)}, u32[]{:S(2)}, u32[]{:S(2)}) collective-permute-start(bf16[320,1024]{1,0:T(8,128)(2,1)} %get-tuple-element.96), channel_id=1, source_target_pairs={{0,3},{1,0},{2,1},{3,2},{4,7},{5,4},{6,5},{7,6},{8,11},{9,8},{10,9... | collective-permute-start | bytes 1966088 | tf_op jit(solution)/shard_map/ppermute | solution.py:56
  93.0 12.5 %collective-permute-start.15 = (bf16[4,2,128,512]{3,2,1,0:T(8,128)(2,1)}, bf16[4,2,128,512]{3,2,1,0:T(8,128)(2,1)S(1)}, u32[]{:S(2)}, u32[]{:S(2)}) collective-permute-start(bf16[4,2,128,512]{3,2,1,0:T(8,128)(2,1)} %get-tuple-element.106), channel_id=1, source_target_pairs={{0,16},{16,0},{32,48},{48,32},{64,80},{80,64},{96,112},{112,96},{1... | collective-permute-start | bytes 3145736 | tf_op jit(solution)/shard_map/ppermute | solution.py:60
  93.0 12.4 %collective-permute-start.16 = (bf16[4,2,128,512]{3,2,1,0:T(8,128)(2,1)}, bf16[4,2,128,512]{3,2,1,0:T(8,128)(2,1)S(1)}, u32[]{:S(2)}, u32[]{:S(2)}) collective-permute-start(bf16[4,2,128,512]{3,2,1,0:T(8,128)(2,1)} %get-tuple-element.107), channel_id=1, source_target_pairs={{0,16},{16,0},{32,48},{48,32},{64,80},{80,64},{96,112},{112,96},{1... | collective-permute-start | bytes 3145736 | tf_op jit(solution)/shard_map/ppermute | solution.py:60
  93.5 13.3 %collective-permute-start.13 = (bf16[320,1024]{1,0:T(8,128)(2,1)S(1)}, bf16[320,1024]{1,0:T(8,128)(2,1)S(1)}, u32[]{:S(2)}, u32[]{:S(2)}) collective-permute-start(bf16[320,1024]{1,0:T(8,128)(2,1)S(1)} %collective-permute-done.11), channel_id=1, source_target_pairs={{0,1},{1,2},{2,3},{3,0},{4,5},{5,6},{6,7},{7,4},{8,9},{9,10},{10,1... | collective-permute-start | bytes 1966088 | tf_op jit(solution)/shard_map/ppermute | solution.py:56
  93.5 13.3 %collective-permute-start.14 = (bf16[320,1024]{1,0:T(8,128)(2,1)S(1)}, bf16[320,1024]{1,0:T(8,128)(2,1)}, u32[]{:S(2)}, u32[]{:S(2)}) collective-permute-start(bf16[320,1024]{1,0:T(8,128)(2,1)S(1)} %collective-permute-done.12), channel_id=1, source_target_pairs={{0,3},{1,0},{2,1},{3,2},{4,7},{5,4},{6,5},{7,6},{8,11},{9,8},{10,9... | collective-permute-start | bytes 1966088 | tf_op jit(solution)/shard_map/ppermute | solution.py:56
  96.8 8.7 %copy-start = (bf16[2,4,2,128,512]{4,3,2,1,0:T(8,128)(2,1)S(1)}, bf16[2,4,2,128,512]{4,3,2,1,0:T(8,128)(2,1)}, u32[]{:S(2)}) copy-start(bf16[2,4,2,128,512]{4,3,2,1,0:T(8,128)(2,1)} %get-tuple-element.105) | copy-start | bytes 6291460
  105.5 1.3 copy-start.8
  105.5 4.1 %copy-start.1 = (bf16[4,2,512,128]{3,2,1,0:T(8,128)(2,1)S(1)}, bf16[4,2,512,128]{3,2,1,0:T(8,128)(2,1)}, u32[]{:S(2)}) copy-start(bf16[4,2,512,128]{3,2,1,0:T(8,128)(2,1)} %get-tuple-element.113) | copy-start | bytes 3145732
  106.8 5.2 %copy-start.3 = (bf16[320,1024]{1,0:T(8,128)(2,1)}, bf16[320,1024]{1,0:T(8,128)(2,1)S(1)}, u32[]{:S(2)}) copy-start(bf16[320,1024]{1,0:T(8,128)(2,1)S(1)} %collective-permute-done.13.refs_3_) | copy-start | bytes 1966084
  106.8 2.7 %collective-permute-start.17 = (bf16[4,2,512,128]{3,2,1,0:T(8,128)(2,1)S(1)}, bf16[4,2,512,128]{3,2,1,0:T(8,128)(2,1)S(1)}, u32[]{:S(2)}, u32[]{:S(2)}) collective-permute-start(bf16[4,2,512,128]{3,2,1,0:T(8,128)(2,1)S(1)} %copy-done.8), channel_id=1, source_target_pairs={{0,16},{16,0},{32,48},{48,32},{64,80},{80,64},{96,112},{112,96},{1... | collective-permute-start | bytes 3145736 | tf_op jit(solution)/shard_map/ppermute | solution.py:60
  106.9 15.1 %collective-permute-start.21 = (bf16[2,2,2,128,512]{4,3,2,0,1:T(8,128)(2,1)}, bf16[2,2,2,128,512]{4,3,2,0,1:T(8,128)(2,1)S(1)}, u32[]{:S(2)}, u32[]{:S(2)}) collective-permute-start(bf16[2,2,2,128,512]{4,3,2,0,1:T(8,128)(2,1)} %add_convert_fusion), channel_id=1, source_target_pairs={{0,32},{16,112},{32,0},{48,80},{64,96},{80,48},{96,64},{112,16},{1... | collective-permute-start | bytes 3145736 | tf_op jit(solution)/shard_map/ppermute | solution.py:60
  110.5 19.4 %collective-permute-start.23 = (bf16[2,2,512,128]{3,2,1,0:T(8,128)(2,1)}, bf16[2,2,512,128]{3,2,1,0:T(8,128)(2,1)}, u32[]{:S(2)}, u32[]{:S(2)}) collective-permute-start(bf16[2,2,512,128]{3,2,1,0:T(8,128)(2,1)} %add_convert_fusion.3), channel_id=1, source_target_pairs={{0,32},{16,112},{32,0},{48,80},{64,96},{80,48},{96,64},{112,16},{1... | collective-permute-start | bytes 1572872 | tf_op jit(solution)/shard_map/ppermute | solution.py:60
  117.7 15.8 %collective-permute-start.18 = (bf16[256,1024]{1,0:T(8,128)(2,1)}, bf16[256,1024]{1,0:T(8,128)(2,1)S(1)}, u32[]{:S(2)}, u32[]{:S(2)}) collective-permute-start(bf16[256,1024]{1,0:T(8,128)(2,1)} %get-tuple-element.122), channel_id=1, source_target_pairs={{0,4},{1,5},{2,6},{3,7},{4,8},{5,9},{6,10},{7,11},{8,12},{9,13},{1... | collective-permute-start | bytes 1572872 | tf_op jit(solution)/shard_map/ppermute | solution.py:56
  118.5 15.2 %collective-permute-start.19 = (bf16[256,1024]{1,0:T(8,128)(2,1)}, bf16[256,1024]{1,0:T(8,128)(2,1)S(1)}, u32[]{:S(2)}, u32[]{:S(2)}) collective-permute-start(bf16[256,1024]{1,0:T(8,128)(2,1)} %get-tuple-element.123), channel_id=1, source_target_pairs={{0,12},{1,13},{2,14},{3,15},{4,0},{5,1},{6,2},{7,3},{8,4},{9,5},{1... | collective-permute-start | bytes 1572872 | tf_op jit(solution)/shard_map/ppermute | solution.py:56
  121.0 13.8 %collective-permute-start.20 = (bf16[256,1024]{1,0:T(8,128)(2,1)}, bf16[256,1024]{1,0:T(8,128)(2,1)S(1)}, u32[]{:S(2)}, u32[]{:S(2)}) collective-permute-start(bf16[256,1024]{1,0:T(8,128)(2,1)} %get-tuple-element.124), channel_id=1, source_target_pairs={{0,8},{1,9},{2,10},{3,11},{4,12},{5,13},{6,14},{7,15},{8,0},{9,1},... | collective-permute-start | bytes 1572872 | tf_op jit(solution)/shard_map/ppermute | solution.py:56
  122.0 12.8 %copy-start.7 = (bf16[256,1024]{1,0:T(8,128)(2,1)S(1)}, bf16[256,1024]{1,0:T(8,128)(2,1)}, u32[]{:S(2)}) copy-start(bf16[256,1024]{1,0:T(8,128)(2,1)} %get-tuple-element.121) | copy-start | bytes 1572868
  122.2 13.8 %collective-permute-start.22 = (bf16[2,2,128,512]{3,2,1,0:T(8,128)(2,1)S(1)}, bf16[2,2,128,512]{3,2,1,0:T(8,128)(2,1)S(1)}, u32[]{:S(2)}, u32[]{:S(2)}) collective-permute-start(bf16[2,2,128,512]{3,2,1,0:T(8,128)(2,1)S(1)} %fusion.1), channel_id=1, source_target_pairs={{0,96},{16,48},{32,64},{48,16},{64,32},{80,112},{96,0},{112,80},{1... | collective-permute-start | bytes 1572872 | tf_op jit(solution)/shard_map/ppermute | solution.py:60
  131.0 7.7 %collective-permute-start.24 = (bf16[2,512,128]{2,1,0:T(8,128)(2,1)S(1)}, bf16[2,512,128]{2,1,0:T(8,128)(2,1)S(1)}, u32[]{:S(2)}, u32[]{:S(2)}) collective-permute-start(bf16[2,512,128]{2,1,0:T(8,128)(2,1)S(1)} %fusion.6), channel_id=1, source_target_pairs={{0,96},{16,48},{32,64},{48,16},{64,32},{80,112},{96,0},{112,80},{1... | collective-permute-start | bytes 786440 | tf_op jit(solution)/shard_map/ppermute | solution.py:60
  (3 other events, 2.5 us)
